TPU v7x, 128 devices: a whole 4x4x4 slice. The times are simulated.
128 devices in a mesh: dp: 4 (over y), ep: 32 (over z, x, core).
Axes of the slice: x: 4, y: 4, z: 4, core: 2. Of those that a mesh axis runs over, the one named last changes fastest.
Arguments:
- residual: bfloat16 [2048, 4096], P(('dp', 'ep')), may hold values from -1.1953125 to 1.1953125
- query: bfloat16 [2048, 4096], P(('dp', 'ep')), may hold values from -6 to 6
- new_key_value: bfloat16 [2048, 2, 256], P(('dp', 'ep')), may hold values from -6 to 6
- cached_key_rows: bfloat16 [2048, 256, 256], P(('dp', 'ep')), may hold values from -64 to 64
- cached_value_rows: bfloat16 [2048, 256, 256], P(('dp', 'ep')), may hold values from -6 to 6
- lengths: int32 [2048], P(('dp', 'ep')), may hold values from 1 to 256, as said below
- q_gain: float32 [128], replicated, may hold values from 0.1 to 1.9
- k_gain: float32 [128], replicated, may hold values from 0.1 to 1.9
- out_weight: bfloat16 [4096, 4096], P(None, 'ep'), may hold values from -0.09375 to 0.09375
- moe_gain: float32 [4096], replicated, may hold values from 0.1 to 1.9
- expert_ids: int32 [2048, 8], P(('dp', 'ep')), may hold values from 0 to 127, all different within a row; in each aligned block of 16 rows (0 to 15, 16 to 31, ...) at most 2 rows name the same one
- gate_probs: float32 [2048, 8], P(('dp', 'ep')), may hold values from 0.02 to 1
- expert_gate_up: bfloat16 [128, 4096, 1536], P(('dp', 'ep')), may hold values from -0.09375 to 0.09375
- expert_down: bfloat16 [128, 768, 4096], P(('dp', 'ep')), may hold values from -0.21875 to 0.21875
Outputs:
- attended: bfloat16 [2048, 4096], P(('dp', 'ep'))
- mixed: bfloat16 [2048, 4096], P(('dp', 'ep'))
Inputs may be any that keep to these rules, and one draw needn't show every extreme that they name: `expert_ids`: each token names 8 different experts; among the 16 tokens of one device no expert is named more than 2 times. `lengths`: some request has exactly 256 live slots in every draw.
All inputs are finite; a program needn't handle non-finite values.
Results may differ from a plain program's by a relative error of at most 0.02.
Values may be sent and summed in bfloat16 or wider, within the bound.
A program may use at most 128 MiB of HBM per device.

v0:
```python
import math

import jax
import jax.numpy as jnp
from jax import lax
from jax.sharding import PartitionSpec as P

EPSILON = 1e-06
THETA = 1000000.0


def head_norm(value_rows, gain):
    mean_square = jnp.mean(value_rows * value_rows, axis=-1, keepdims=True)
    return value_rows * lax.rsqrt(mean_square + EPSILON) * gain


def rotate(value_rows, positions):
    width = value_rows.shape[-1]
    half = width // 2
    steps = jnp.arange(half).astype(jnp.float32)
    freqs = jnp.exp(steps * (-2.0 * math.log(THETA) / width))
    angles = positions[..., None] * freqs
    cosines = jnp.cos(angles)
    sines = jnp.sin(angles)
    first_part = value_rows[..., :half]
    second_part = value_rows[..., half:]
    return jnp.concatenate(
        [first_part * cosines - second_part * sines, second_part * cosines + first_part * sines],
        axis=-1,
    )


def attend_block(query, new_key_value, cached_key_rows, cached_value_rows, lengths, q_gain, k_gain):
    head = q_gain.shape[0]
    count = query.shape[0]
    kv_heads = new_key_value.shape[2] // head
    group = query.shape[1] // head // kv_heads
    slots = cached_key_rows.shape[1]
    positions = lengths.astype(jnp.float32)
    queries = query.astype(jnp.float32).reshape(count, kv_heads, group, head)
    queries = rotate(head_norm(queries, q_gain), positions[:, None, None]).astype(jnp.bfloat16)
    new_key = new_key_value[:, 0].astype(jnp.float32).reshape(count, kv_heads, head)
    new_key = rotate(head_norm(new_key, k_gain), positions[:, None]).astype(jnp.bfloat16)
    new_value = new_key_value[:, 1].reshape(count, kv_heads, head)
    stored_keys = cached_key_rows.reshape(count, slots, kv_heads, head)
    stored_values = cached_value_rows.reshape(count, slots, kv_heads, head)
    scale = 1.0 / math.sqrt(head)
    scores = (
        jnp.einsum("tkgd,tckd->tkgc", queries, stored_keys, preferred_element_type=jnp.float32)
        * scale
    )
    own_score = (
        jnp.einsum("tkgd,tkd->tkg", queries, new_key, preferred_element_type=jnp.float32) * scale
    )
    live = (jnp.arange(slots)[None, :] < lengths[:, None])[:, None, None, :]
    scores = jnp.where(live, scores, -jnp.inf)
    highest = jnp.maximum(jnp.max(scores, axis=-1), own_score)
    expos = jnp.where(live, jnp.exp(scores - highest[..., None]), 0.0)
    own_expo = jnp.exp(own_score - highest)
    total = jnp.sum(expos, axis=-1) + own_expo
    probs = (expos / total[..., None]).astype(jnp.bfloat16)
    own_prob = (own_expo / total).astype(jnp.bfloat16)
    summed = jnp.einsum("tkgc,tckd->tkgd", probs, stored_values, preferred_element_type=jnp.float32)
    summed = (
        summed
        + own_prob.astype(jnp.float32)[..., None] * new_value.astype(jnp.float32)[:, :, None, :]
    )
    return summed.astype(jnp.bfloat16).reshape(count, kv_heads * group * head)


def expert_rows(rows, gate_up, down):
    hidden_size = down.shape[0]
    both = jnp.dot(rows, gate_up, preferred_element_type=jnp.float32)
    activated = (jax.nn.silu(both[:, :hidden_size]) * both[:, hidden_size:]).astype(jnp.bfloat16)
    return jnp.dot(activated, down, preferred_element_type=jnp.float32)


def local(
    residual,
    query,
    new_key_value,
    cached_key_rows,
    cached_value_rows,
    lengths,
    q_gain,
    k_gain,
    out_weight,
    moe_gain,
    expert_ids,
    gate_probs,
    expert_gate_up,
    expert_down,
):
    head_list = attend_block(
        query, new_key_value, cached_key_rows, cached_value_rows, lengths, q_gain, k_gain
    )
    gathered = jnp.dot(
        lax.all_gather(head_list, "ep", axis=0, tiled=True),
        out_weight,
        preferred_element_type=jnp.float32,
    ).astype(jnp.bfloat16)
    projected = lax.all_to_all(gathered, "ep", split_axis=0, concat_axis=1, tiled=True)
    attended = (residual.astype(jnp.float32) + projected.astype(jnp.float32)).astype(jnp.bfloat16)
    stream = attended.astype(jnp.float32)
    normed = (
        stream * lax.rsqrt(jnp.mean(stream * stream, axis=-1, keepdims=True) + EPSILON) * moe_gain
    ).astype(jnp.bfloat16)
    weights = gate_probs / jnp.sum(gate_probs, axis=-1, keepdims=True)
    tok_count, top_count = expert_ids.shape
    width = residual.shape[1]
    dp_size = lax.axis_size("dp")
    ep_size = lax.axis_size("ep")
    owner_count = dp_size * ep_size
    capacity = max(2, tok_count * top_count * 2 // owner_count)
    flat_ids = expert_ids.reshape(-1)
    matches = (flat_ids[:, None] == jnp.arange(owner_count, dtype=jnp.int32)[None, :]).astype(
        jnp.int32
    )
    earlier = jnp.cumsum(matches, axis=0) - matches
    slots = jnp.sum(earlier * matches, axis=1)
    targets = flat_ids * capacity + slots
    placing = (
        jnp.arange(owner_count * capacity, dtype=jnp.int32)[:, None, None]
        == targets.reshape(tok_count, top_count)[None]
    ).astype(jnp.int32)
    placing = jnp.sum(placing, axis=2).astype(jnp.bfloat16)
    outgoing = jnp.dot(placing, normed, preferred_element_type=jnp.float32).astype(jnp.bfloat16)
    outgoing = outgoing.reshape(owner_count, capacity, width)
    gate_up = expert_gate_up[0]
    down = expert_down[0]
    rows = lax.all_to_all(outgoing, ("dp", "ep"), split_axis=0, concat_axis=0, tiled=True)
    sources, items, row_width = rows.shape
    result = expert_rows(rows.reshape(sources * items, row_width), gate_up, down)
    answers = result.reshape(sources, items, row_width)
    returned = lax.all_to_all(
        answers.astype(jnp.bfloat16), ("dp", "ep"), split_axis=0, concat_axis=0, tiled=True
    ).astype(answers.dtype)
    returned = returned.reshape(owner_count * capacity, width)
    picked = returned[targets].reshape(tok_count, top_count, width)
    moe_out = jnp.sum(weights[:, :, None] * picked, axis=1)
    mixed = (stream + moe_out).astype(jnp.bfloat16)
    return (attended, mixed)


def solution(mesh):
    return jax.shard_map(
        local,
        mesh=mesh,
        in_specs=(
            P(("dp", "ep"), None),
            P(("dp", "ep"), None),
            P(("dp", "ep"), None, None),
            P(("dp", "ep"), None, None),
            P(("dp", "ep"), None, None),
            P(("dp", "ep")),
            P(),
            P(),
            P(None, "ep"),
            P(),
            P(("dp", "ep"), None),
            P(("dp", "ep"), None),
            P(("dp", "ep"), None, None),
            P(("dp", "ep"), None, None),
        ),
        out_specs=(P(("dp", "ep"), None), P(("dp", "ep"), None)),
        check_vma=False,
    )
```

profile of v0, /device:TPU:1, one launch (start us, length us, event | category | flops | bytes accessed | tf_op | source)
XLA Modules:
  0.0 201.7 jit_solution(17332655343879684657)
XLA Ops:
  7.2 0.8 convert_element_type.98
  8.0 0.7 iota_compare_fusion.2
  8.8 0.8 slice_convert_fusion
  9.6 0.1 multiply_reduce_fusion.1
  9.7 0.9 convert_bitcast_fusion.1
  10.6 0.1 copy.52
  10.7 0.2 multiply_reduce_fusion
  10.9 0.7 multiply_multiply_fusion.1
  11.6 0.1 multiply_cosine_fusion
  11.7 0.8 multiply_multiply_fusion
  12.5 0.1 subtract_convert_fusion.1
  12.6 0.1 subtract_convert_fusion
  12.8 0.1 maximum_bitcast_fusion
  12.9 0.2 fusion.42
  13.2 0.8 fusion.53
  14.0 0.3 fusion.27
  14.3 0.1 copy-done.6
  14.4 0.5 fusion.23
  14.9 0.7 copy.79
  15.6 0.1 copy.43
  15.7 0.1 eq.29
  15.8 0.1 fusion.41
  15.9 0.2 reduce_window_sum.11
  16.0 0.2 select_reduce_fusion
  16.2 0.1 reduce_sum.81
  16.3 49.4 %all-gather.2.cloned.1.call-done = bf16[512,4096]{1,0:T(8,128)(2,1)} async-done(((bf16[16,4096]{1,0:T(8,128)(2,1)}), bf16[512,4096]{1,0:T(8,128)(2,1)}) %all-gather.2.cloned.1.call-update) | async-done | bytes 4194320 | tf_op jit(solution)/shard_map/all_gather | solution.py:98
  65.8 4.4 %convolution_convert_fusion.1 = bf16[512,128]{1,0:T(8,128)(2,1)} fusion(bf16[512,4096]{1,0:T(8,128)(2,1)} %all-gather.2.cloned.1.call-done, bf16[4096,128]{1,0:T(8,128)(2,1)} %param.22), kind=kOutput, calls=%fused_computation.19 | convolution fusion | flops 536936448 | bytes 5373952 | tf_op jit(solution)/shard_map/dot_general | solution.py:97
  70.2 5.3 %all-to-all-start = ((bf16[32,16,128]{2,1,0:T(8,128)(2,1)}), bf16[32,16,128]{2,1,0:T(8,128)(2,1)S(1)}, u32[]{:S(2)}, u32[]{:S(2)}) async-start(bf16[32,16,128]{2,1,0:T(8,128)(2,1)} %bitcast.5), calls=%async_computation | async-start | bytes 262144 | tf_op jit(solution)/shard_map/all_to_all | solution.py:102
  75.5 0.1 convert_reduce_fusion
  75.6 7.5 %all-to-all-done = bf16[32,16,128]{2,1,0:T(8,128)(2,1)S(1)} async-done(((bf16[32,16,128]{2,1,0:T(8,128)(2,1)}), bf16[32,16,128]{2,1,0:T(8,128)(2,1)S(1)}, u32[]{:S(2)}, u32[]{:S(2)}) %all-to-all-start) | async-done | bytes 131104 | tf_op jit(solution)/shard_map/all_to_all | solution.py:102
  83.1 0.2 fusion.29
  83.3 2.0 %convolution_convert_fusion = bf16[256,4096]{1,0:T(8,128)(2,1)} fusion(bf16[16,4096]{1,0:T(8,128)(2,1)S(1)} %get-tuple-element.3, f32[4096]{0:T(1024)S(1)} %copy-done.3, f32[16]{0:T(128)S(1)} %add_rsqrt_fusion.2, s32[256,16]{0,1:T(8,128)S(1)} %convert_reduce_fusion), kind=kOutput, calls=%fused_computation.5 | convolution fusion | flops 34869248 | bytes 2261056 | tf_op jit(solution)/shard_map/dot_general | solution.py:127
  85.3 4.4 %reshape.262 = bf16[128,2,4096]{2,1,0:T(2,128)(2,1)} reshape(bf16[256,4096]{1,0:T(8,128)(2,1)} %convolution_convert_fusion) | data formatting | bytes 4194304 | tf_op jit(solution)/shard_map/reshape | solution.py:128
  89.7 36.4 %all_to_all.23 = bf16[128,2,4096]{2,1,0:T(2,128)(2,1)} all-to-all(bf16[128,2,4096]{2,1,0:T(2,128)(2,1)} %reshape.262), channel_id=1, replica_groups=mesh['dp'=4,'ep'=32] {'dp','ep'}, dimensions={0} | all-to-all | bytes 4194304 | tf_op jit(solution)/shard_map/all_to_all | solution.py:131
  126.1 4.1 %reshape.263 = bf16[256,4096]{1,0:T(8,128)(2,1)} reshape(bf16[128,2,4096]{2,1,0:T(2,128)(2,1)} %all_to_all.23) | data formatting | bytes 4194304 | tf_op jit(solution)/shard_map/reshape | solution.py:133
  130.2 7.0 %fusion = f32[256,1536]{1,0:T(8,128)S(1)} fusion(bf16[256,4096]{1,0:T(8,128)(2,1)} %reshape.263, bf16[1,4096,1536]{2,1,0:T(8,128)(2,1)} %param.26), kind=kOutput, calls=%fused_computation.1 | convolution fusion | flops 3221225472 | bytes 16252928 | tf_op jit(solution)/shard_map/dot_general | solution.py:73
  137.2 0.2 fusion.26
  137.5 0.1 dot_general.29
  137.6 4.6 %fusion.4 = bf16[128,2,4096]{2,0,1:T(8,128)(2,1)S(1)} fusion(bf16[1,768,4096]{2,1,0:T(8,128)(2,1)} %param.27, bf16[128,2,768]{2,1,0:T(2,128)(2,1)S(1)} %dot_general.29), kind=kOutput, calls=%fused_computation.6 | convolution fusion | flops 1611661312 | bytes 8781824 | tf_op jit(solution)/shard_map/dot_general | solution.py:75
  142.2 3.5 %copy.46 = bf16[128,2,4096]{2,1,0:T(2,128)(2,1)} copy(bf16[128,2,4096]{2,0,1:T(8,128)(2,1)S(1)} %fusion.4) | data formatting | bytes 4194304 | tf_op jit(solution)/shard_map/convert_element_type | solution.py:136
  145.8 5.7 %all-to-all-start.2 = ((bf16[128,2,4096]{2,1,0:T(2,128)(2,1)}), bf16[128,2,4096]{2,1,0:T(2,128)(2,1)}, u32[]{:S(2)}, u32[]{:S(2)}) async-start(bf16[128,2,4096]{2,1,0:T(2,128)(2,1)} %copy.46), calls=%async_computation.2 | async-start | bytes 4194304 | tf_op jit(solution)/shard_map/all_to_all | solution.py:135
  151.5 0.1 mul.270
  151.6 0.1 copy.42
  151.7 30.1 %all-to-all-done.2 = bf16[128,2,4096]{2,1,0:T(2,128)(2,1)} async-done(((bf16[128,2,4096]{2,1,0:T(2,128)(2,1)}), bf16[128,2,4096]{2,1,0:T(2,128)(2,1)}, u32[]{:S(2)}, u32[]{:S(2)}) %all-to-all-start.2) | async-done | bytes 2097184 | tf_op jit(solution)/shard_map/all_to_all | solution.py:135
  181.8 4.4 %reshape.273 = f32[256,4096]{1,0:T(8,128)} reshape(bf16[128,2,4096]{2,1,0:T(2,128)(2,1)} %all-to-all-done.2) | data formatting | bytes 6291456 | tf_op jit(solution)/shard_map/reshape | solution.py:138
  186.2 5.6 %gather_fusion = f32[128,4096]{1,0:T(8,128)} fusion(f32[256,4096]{1,0:T(8,128)} %reshape.273, s32[1024]{0:T(1024)S(1)} %pad_clamp_fusion), kind=kCustom, calls=%fused_computation | custom fusion | bytes 4194816 | tf_op jit(solution)/shard_map/gather | solution.py:139
  191.8 2.3 %fusion.13 = f32[16,4096]{1,0:T(8,128)S(1)} fusion(f32[128,4096]{1,0:T(8,128)} %gather_fusion, f32[16,8]{1,0:T(8,128)S(1)} %copy.42), kind=kLoop, calls=%fused_computation.14 | loop fusion | flops 983040 | bytes 2359808 | tf_op jit(solution)/shard_map/reduce_sum | solution.py:140
  194.1 0.7 fusion.32
  (26 shorter events, 0.2 us)
Async XLA Ops:
  7.2 6.0 %copy-start = (bf16[16,256,256]{2,1,0:T(8,128)(2,1)S(1)}, bf16[16,256,256]{2,1,0:T(8,128)(2,1)}, u32[]{:S(2)}) copy-start(bf16[16,256,256]{2,1,0:T(8,128)(2,1)} %param.17) | copy-start | bytes 6291460
  7.2 58.6 %all-gather.2.cloned.1.call-start = ((), (), s32[]{:S(2)}) async-start(), calls=%async_computation.3 | async-start | bytes 4325376 | tf_op jit(solution)/shard_map/all_gather | solution.py:98
  12.8 1.6 copy-start.6
  14.4 1.2 copy-start.5
  16.3 66.8 %copy-start.2 = (bf16[16,4096]{1,0:T(8,128)(2,1)S(1)}, bf16[16,4096]{1,0:T(8,128)(2,1)}, u32[]{:S(2)}) copy-start(bf16[16,4096]{1,0:T(8,128)(2,1)} %param.14) | copy-start | bytes 393220
  16.3 66.9 %copy-start.3 = (f32[4096]{0:T(1024)S(1)}, f32[4096]{0:T(1024)}, u32[]{:S(2)}) copy-start(f32[4096]{0:T(1024)} %param.23) | copy-start | bytes 49156
  70.2 12.9 %all-to-all-start = ((bf16[32,16,128]{2,1,0:T(8,128)(2,1)}), bf16[32,16,128]{2,1,0:T(8,128)(2,1)S(1)}, u32[]{:S(2)}, u32[]{:S(2)}) async-start(bf16[32,16,128]{2,1,0:T(8,128)(2,1)} %bitcast.5), calls=%async_computation | async-start | bytes 262144 | tf_op jit(solution)/shard_map/all_to_all | solution.py:102
  83.2 110.9 %copy-start.1 = (bf16[16,4096]{1,0:T(8,128)(2,1)}, bf16[16,4096]{1,0:T(8,128)(2,1)S(1)}, u32[]{:S(2)}) copy-start(bf16[16,4096]{1,0:T(8,128)(2,1)S(1)} %get-tuple-element.3) | copy-start | bytes 393220
  145.8 5.8 %copy-start.4 = (f32[16,8]{0,1:T(8,128)S(1)}, f32[16,8]{0,1:T(8,128)}, u32[]{:S(2)}) copy-start(f32[16,8]{0,1:T(8,128)} %param.25) | copy-start | bytes 1540
  145.8 36.1 %all-to-all-start.2 = ((bf16[128,2,4096]{2,1,0:T(2,128)(2,1)}), bf16[128,2,4096]{2,1,0:T(2,128)(2,1)}, u32[]{:S(2)}, u32[]{:S(2)}) async-start(bf16[128,2,4096]{2,1,0:T(2,128)(2,1)} %copy.46), calls=%async_computation.2 | async-start | bytes 4194304 | tf_op jit(solution)/shard_map/all_to_all | solution.py:135
Sparse Core Ops, SparseCore 0:
  15.7 49.9 all-gather.1
where the time goes:
time: 202 us
  waiting for transfers between devices  87 us (43%)
  blocking collectives  36.4 us (18%)
  local copies, waits for them, and re-layouts  23.5 us (12%)
  matrix products  19.6 us (10%)
  between operations  14.3 us (7%)
  starting transfers between devices  11.1 us (5%)
  other arithmetic  9.83 us (5%)
    all_gather x1, waiting for transfers between devices, local(): lax.all_gather(head_list, 'ep', axis=0, tiled=True)  49.4 us
    all_to_all x1, blocking collectives, local(): lax.all_to_all(outgoing, ('dp', 'ep'), split_axis=0, concat_axis=0, tiled...  36.4 us
    all_to_all x1, waiting for transfers between devices, local(): lax.all_to_all(answers.astype(jnp.bfloat16), ('dp', 'ep'), split_axis=0,...  30.1 us
    all_to_all x1, waiting for transfers between devices, local(): lax.all_to_all(gathered, 'ep', split_axis=0, concat_axis=1, tiled=True)  7.5 us
    dot_general x1, matrix products, expert_rows(): both = jnp.dot(rows, gate_up, preferred_element_type=jnp.float32)  7.02 us
    all_to_all x1, starting transfers between devices, local(): lax.all_to_all(answers.astype(jnp.bfloat16), ('dp', 'ep'), split_axis=0,...  5.74 us
    gather x1, local copies, waits for them, and re-layouts, local(): picked = returned[targets].reshape(tok_count, top_count, width)  5.63 us
    all_to_all x1, starting transfers between devices, local(): lax.all_to_all(gathered, 'ep', split_axis=0, concat_axis=1, tiled=True)  5.27 us
  transfers between devices with their start and end apart: 3, of which 3 were waited for; matrix products, arithmetic and copies ran while one was open for 0% of the time, Pallas kernels for 0%

commit v1 on v0

--- a/solution.py
+++ b/solution.py
@@ -3,6 +3,8 @@
 import jax
 import jax.numpy as jnp
 from jax import lax
+from jax.experimental import pallas as pl
+from jax.experimental.pallas import tpu as pltpu
 from jax.sharding import PartitionSpec as P
 
 EPSILON = 1e-06
@@ -68,11 +70,566 @@
     return summed.astype(jnp.bfloat16).reshape(count, kv_heads * group * head)
 
 
-def expert_rows(rows, gate_up, down):
-    hidden_size = down.shape[0]
-    both = jnp.dot(rows, gate_up, preferred_element_type=jnp.float32)
-    activated = (jax.nn.silu(both[:, :hidden_size]) * both[:, hidden_size:]).astype(jnp.bfloat16)
-    return jnp.dot(activated, down, preferred_element_type=jnp.float32)
+MESH = pl.DeviceIdType.MESH
+SIDE = 4
+CHUNKS = 4
+
+
+def place():
+    y = lax.axis_index("dp")
+    e = lax.axis_index("ep")
+    return (e // 2) % SIDE, y, e // (2 * SIDE), e % 2
+
+
+def device(x, y, z, core):
+    return (y, (z * SIDE + x) * 2 + core)
+
+
+def signal(target):
+    pl.semaphore_signal(
+        pltpu.get_barrier_semaphore(), inc=1, device_id=target, device_id_type=MESH
+    )
+
+
+def send(source, target, send_sem, recv_sem, where):
+    pltpu.make_async_remote_copy(
+        src_ref=source,
+        dst_ref=target,
+        send_sem=send_sem,
+        recv_sem=recv_sem,
+        device_id=where,
+        device_id_type=MESH,
+    ).start()
+
+
+def wait(ref, sem):
+    pltpu.make_async_copy(ref, ref, sem).wait()
+
+
+def loop(first, last, body):
+    def step(i, carry):
+        body(i)
+        return carry
+
+    lax.fori_loop(first, last, step, 0)
+
+
+def near_first(i):
+    return 1 + 2 * i - 3 * (i // 2)
+
+
+def project_kernel(
+    heads, residual, weight, gain, attended, normed, columns, blocks, products, projected,
+    weight_sems, first_send, first_recv, second_send, second_recv, back_send, back_recv,
+):
+    x, y, z, core = place()
+    first = x * (1 - core) + z * core
+    second = z * (1 - core) + x * core
+
+    def at(f, s):
+        return device(f * (1 - core) + s * core, y, s * (1 - core) + f * core, core)
+
+    sibling = device(x, y, z, 1 - core)
+    signal(sibling)
+
+    def greet(i):
+        other = (second * SIDE + first + i) % (SIDE * SIDE)
+        signal(at(other % SIDE, other // SIDE))
+
+    loop(1, SIDE * SIDE, greet)
+    half = pl.ds(pl.multiple_of(core * 128, 128), 128)
+    own_weight = pltpu.make_async_copy(weight, columns.at[:, half], weight_sems.at[0])
+    own_weight.start()
+    blocks[second, first] = heads[...]
+    pl.semaphore_wait(pltpu.get_barrier_semaphore(), SIDE * SIDE)
+
+    def start_first(i):
+        f = (first + near_first(i)) % SIDE
+        send(heads, blocks.at[second, first], first_send.at[f], first_recv.at[first], at(f, second))
+
+    loop(0, SIDE - 1, start_first)
+
+    def start_second(f):
+        def one(i):
+            s = (second + near_first(i)) % SIDE
+            send(
+                blocks.at[second, f], blocks.at[second, f], second_send.at[s, f],
+                second_recv.at[second, f], at(first, s),
+            )
+
+        loop(0, SIDE - 1, one)
+
+    start_second(first)
+    send(weight, columns.at[:, half], weight_sems.at[1], weight_sems.at[2], sibling)
+
+    def pass_on(i):
+        f = (first + near_first(i)) % SIDE
+        wait(blocks.at[second, f], first_recv.at[f])
+        start_second(f)
+
+    loop(0, SIDE - 1, pass_on)
+    own_weight.wait()
+    wait(weight, weight_sems.at[2])
+    mine = pl.ds(pl.multiple_of((z * SIDE + x) * 256, 256), 256)
+
+    def group(s):
+        rows = blocks[s].reshape(SIDE * 16, blocks.shape[3])
+        result = jnp.dot(rows, columns[...], preferred_element_type=jnp.float32)
+        products[s] = result.astype(jnp.bfloat16).reshape(SIDE, 16, 256)
+
+    def back(f, s):
+        send(
+            products.at[s, f], projected.at[:, mine], back_send.at[s, f],
+            back_recv.at[second, first], at(f, s),
+        )
+
+    group(second)
+    projected[:, mine] = products[second, first]
+    loop(0, SIDE - 1, lambda i: back((first + near_first(i)) % SIDE, second))
+
+    def other_group(i):
+        s = (second + near_first(i)) % SIDE
+        loop(0, SIDE, lambda f: wait(blocks.at[s, f], second_recv.at[s, f]))
+        group(s)
+        loop(0, SIDE, lambda f: back(f, s))
+
+    loop(0, SIDE - 1, other_group)
+
+    def collect(i):
+        other = (second * SIDE + first + i) % (SIDE * SIDE)
+        f, s = other % SIDE, other // SIDE
+        wait(products.at[s, f], back_recv.at[s, f])
+
+    loop(1, SIDE * SIDE, collect)
+    total = residual[...].astype(jnp.float32) + projected[...].astype(jnp.float32)
+    rounded = total.astype(jnp.bfloat16)
+    attended[...] = rounded
+    stream = rounded.astype(jnp.float32)
+    level = lax.rsqrt(jnp.mean(stream * stream, axis=-1, keepdims=True) + EPSILON)
+    normed[...] = (stream * level * gain[...]).astype(jnp.bfloat16)
+
+    wait(weight, weight_sems.at[1])
+
+    def finish_first(i):
+        f = (first + 1 + i) % SIDE
+        wait(heads, first_send.at[f])
+
+        def finish_second(g):
+            s = (second + 1 + i) % SIDE
+            wait(blocks.at[second, g], second_send.at[s, g])
+
+        loop(0, SIDE, finish_second)
+
+    loop(0, SIDE - 1, finish_first)
+
+    def finish_back(i):
+        other = (second * SIDE + first + i) % (SIDE * SIDE)
+        f, s = other % SIDE, other // SIDE
+        wait(products.at[s, f], back_send.at[s, f])
+
+    loop(1, SIDE * SIDE, finish_back)
+
+
+def project(heads, residual, weight, gain):
+    rows, width = heads.shape
+    vmem = pl.BlockSpec(memory_space=pltpu.VMEM)
+    sems = pltpu.SemaphoreType.DMA
+    return pl.pallas_call(
+        project_kernel,
+        out_shape=[jax.ShapeDtypeStruct((rows, width), jnp.bfloat16)] * 2,
+        in_specs=[vmem, vmem, pl.BlockSpec(memory_space=pl.ANY), vmem],
+        out_specs=[vmem, vmem],
+        scratch_shapes=[
+            pltpu.VMEM((width, 256), jnp.bfloat16),
+            pltpu.VMEM((SIDE, SIDE, rows, width), jnp.bfloat16),
+            pltpu.VMEM((SIDE, SIDE, rows, 256), jnp.bfloat16),
+            pltpu.VMEM((rows, width), jnp.bfloat16),
+            sems((3,)),
+            sems((SIDE,)),
+            sems((SIDE,)),
+            sems((SIDE, SIDE)),
+            sems((SIDE, SIDE)),
+            sems((SIDE, SIDE)),
+            sems((SIDE, SIDE)),
+        ],
+        compiler_params=pltpu.CompilerParams(
+            collective_id=1, has_side_effects=True, vmem_limit_bytes=24 << 20
+        ),
+        name="project",
+    )(heads, residual, weight, gain)
+
+
+def route(ids, probs):
+    count, top = ids.shape
+    experts = 128
+    weights = probs / jnp.sum(probs, axis=-1, keepdims=True)
+    label = lax.broadcasted_iota(jnp.int32, (count, experts), 1)
+    named = jnp.zeros((count, experts), jnp.float32)
+    value = jnp.zeros((count, experts), jnp.float32)
+    for k in range(top):
+        match = ids[:, k : k + 1] == label
+        named = named + jnp.where(match, 1.0, 0.0)
+        value = value + jnp.where(match, weights[:, k : k + 1], 0.0)
+    below = lax.broadcasted_iota(jnp.int32, (count, count), 1) < lax.broadcasted_iota(
+        jnp.int32, (count, count), 0
+    )
+    earlier = jnp.dot(
+        jnp.where(below, 1.0, 0.0), named, preferred_element_type=jnp.float32
+    )
+    again = earlier > 0.5
+    return jnp.concatenate(
+        [jnp.where(again, 0.0, value), jnp.where(again, value, 0.0)], axis=1
+    ).astype(jnp.bfloat16)
+
+
+def experts_kernel(
+    normed, attended, ids, probs, gate_up, down, mixed,
+    gate_up_held, down_held, meta, rows_held, picked, received, total, answers, returned,
+    partial, landed, summed, landed_last, choose, weigh,
+    weight_sems, meta_sems, a_send, a_recv, b_send, b_recv, out_send, out_recv,
+    ret_send, ret_recv, c_send, c_recv, d_send, d_recv,
+):
+    x, y, z, core = place()
+    first = x * (1 - core) + z * core
+    line = z * (1 - core) + x * core
+    width = normed.shape[1]
+    size = width // CHUNKS
+    last = CHUNKS - 1
+
+    def at(f, row, l, c):
+        return device(f * (1 - core) + l * core, row, l * (1 - core) + f * core, c)
+
+    def peer_first(f):
+        return at(f, y, line, core)
+
+    def peer_row(row):
+        return at(first, row, line, core)
+
+    def expert_at(e):
+        return at(first, y, e // 2, e % 2)
+
+    def source_at(q):
+        c = q // SIDE
+        l = q % SIDE
+        return device(x * (1 - c) + l * c, y, l * (1 - c) + z * c, c)
+
+    own_expert = line * 2 + core
+    own_source = core * SIDE + line
+    def answer_slot(q):
+        c = q // SIDE
+        return (z * (1 - c) + x * c) * 2 + core
+
+    def cols(j):
+        return pl.ds(pl.multiple_of(j * size, size), size)
+
+    def others(body):
+        loop(0, SIDE - 1, lambda i: body(near_first(i)))
+
+    others(lambda d: signal(peer_first((first + d) % SIDE)))
+    others(lambda d: signal(peer_row((y + d) % SIDE)))
+    loop(1, 2 * SIDE, lambda i: signal(expert_at((own_expert + i) % (2 * SIDE))))
+    loop(1, 2 * SIDE, lambda i: signal(source_at((own_source + i) % (2 * SIDE))))
+
+    def fetch_gate_up(j):
+        part = pl.ds(pl.multiple_of(j * size, size), size)
+        return pltpu.make_async_copy(
+            gate_up.at[0, part], gate_up_held.at[part], weight_sems.at[j]
+        )
+
+    def fetch_down(j):
+        return pltpu.make_async_copy(
+            down.at[0, :, cols(j)], down_held.at[:, cols(j)], weight_sems.at[CHUNKS + j]
+        )
+
+    loop(0, CHUNKS, lambda j: fetch_gate_up(j).start())
+    loop(0, CHUNKS, lambda j: fetch_down(j).start())
+    meta[y, first] = route(ids[...], probs[...])
+    rows_held[y, first] = normed[...]
+    pl.semaphore_wait(pltpu.get_barrier_semaphore(), 2 * (SIDE - 1) + 2 * (2 * SIDE - 1))
+
+    def to_first(ref, slot, send_sem, recv_sem):
+        def one(d):
+            f = (first + d) % SIDE
+            send(ref, slot, send_sem.at[f], recv_sem.at[first], peer_first(f))
+
+        others(one)
+
+    def to_rows(ref, slot, send_sem, recv_sem):
+        def one(d):
+            row = (y + d) % SIDE
+            send(ref, slot, send_sem.at[row], recv_sem.at[y], peer_row(row))
+
+        others(one)
+
+    def wait_others(ref, own, sem):
+        others(lambda d: wait(ref, sem.at[(own + d) % SIDE]))
+
+    to_first(meta.at[y, first], meta.at[y, first], meta_sems.at[0], meta_sems.at[1])
+    to_rows(
+        normed.at[:, cols(last)], rows_held.at[y, first, :, cols(last)],
+        a_send.at[last], a_recv.at[last],
+    )
+
+    def start_a(j):
+        to_first(
+            normed.at[:, cols(j)], rows_held.at[y, first, :, cols(j)], a_send.at[j], a_recv.at[j]
+        )
+
+    loop(0, last, start_a)
+    wait_others(meta.at[y, first], first, meta_sems.at[1])
+    to_rows(meta.at[y], meta.at[y], meta_sems.at[2], meta_sems.at[3])
+
+    def start_b(j):
+        wait_others(normed.at[:, cols(j)], first, a_recv.at[j])
+        to_rows(
+            rows_held.at[y, :, :, cols(j)], rows_held.at[y, :, :, cols(j)],
+            b_send.at[j], b_recv.at[j],
+        )
+
+    start_b(0)
+    wait_others(normed.at[:, cols(last)], y, a_recv.at[last])
+    to_first(
+        rows_held.at[:, first, :, cols(last)], rows_held.at[:, first, :, cols(last)],
+        b_send.at[last], b_recv.at[last],
+    )
+    loop(1, last, start_b)
+
+    wait_others(meta.at[y], y, meta_sems.at[3])
+    tokens = SIDE * SIDE * 16
+    known = meta[...].reshape(tokens, 256)
+    row = lax.broadcasted_iota(jnp.int32, (tokens, 256), 0)
+    lane = lax.broadcasted_iota(jnp.int32, (tokens, 256), 1)
+    slot = row % 2
+    expert = row // 32
+    expert_x = x * (1 - core) + (expert // 2) * core
+    expert_z = (expert // 2) * (1 - core) + z * core
+    number = y * 32 + (expert_z * SIDE + expert_x) * 2 + expert % 2
+    wanted = jnp.where(lane == slot * 128 + number, 1.0, 0.0).astype(jnp.bfloat16)
+    nt = (((1,), (1,)), ((), ()))
+    same = (row // 2) % 16 == lane // 16
+    present = jnp.where(known.astype(jnp.float32) > 0.0, 1.0, 0.0).astype(jnp.bfloat16)
+    chosen = lax.dot_general(wanted, present, nt, preferred_element_type=jnp.float32)
+    choose[...] = jnp.where(same, chosen, 0.0).astype(jnp.bfloat16)
+    same_back = row // 16 == (lane // 2) % 16
+    scaled = lax.dot_general(known, wanted, nt, preferred_element_type=jnp.float32)
+    weigh[...] = jnp.where(same_back, scaled, 0.0).astype(jnp.bfloat16)
+
+    def pick(j):
+        plane = rows_held[:, :, :, cols(j)].reshape(tokens, size)
+        result = jnp.dot(choose[...], plane, preferred_element_type=jnp.float32)
+        picked[:, :, cols(j)] = result.astype(jnp.bfloat16).reshape(2 * SIDE, 32, size)
+
+        def one(i):
+            e = (own_expert + i) % (2 * SIDE)
+            send(
+                picked.at[e, :, cols(j)], received.at[own_source, :, cols(j)],
+                out_send.at[j, e], out_recv.at[j, own_source], expert_at(e),
+            )
+
+        loop(1, 2 * SIDE, one)
+        received[own_source, :, cols(j)] = picked[own_expert, :, cols(j)]
+
+    wait_others(rows_held.at[:, first, :, cols(last)], first, b_recv.at[last])
+    pick(last)
+
+    def finish_b(j):
+        wait_others(rows_held.at[y, :, :, cols(j)], y, b_recv.at[j])
+        pick(j)
+
+    loop(0, last, finish_b)
+
+    hidden_size = down.shape[1]
+
+    def expand(i):
+        j = (last + i) % CHUNKS
+
+        def arrived(k):
+            q = (own_source + k) % (2 * SIDE)
+            wait(received.at[q, :, cols(j)], out_recv.at[j, q])
+
+        loop(1, 2 * SIDE, arrived)
+        fetch_gate_up(j).wait()
+        part = pl.ds(pl.multiple_of(j * size, size), size)
+        rows = received[:, :, cols(j)].reshape(tokens, size)
+
+        def columns(n):
+            piece = pl.ds(pl.multiple_of(n * 512, 512), 512)
+            product = jnp.dot(rows, gate_up_held[part, piece], preferred_element_type=jnp.float32)
+
+            @pl.when(i == 0)
+            def _():
+                total[:, piece] = product
+
+            @pl.when(i > 0)
+            def _():
+                total[:, piece] += product
+
+        loop(0, 2 * hidden_size // 512, columns)
+
+    loop(0, CHUNKS, expand)
+    gate = total[:, :hidden_size]
+    hidden = (gate / (1.0 + jnp.exp(-gate)) * total[:, hidden_size:]).astype(jnp.bfloat16)
+
+    def answer(j):
+        fetch_down(j).wait()
+        result = jnp.dot(hidden, down_held[:, cols(j)], preferred_element_type=jnp.float32)
+        answers[:, :, cols(j)] = result.astype(jnp.bfloat16).reshape(2 * SIDE, 32, size)
+
+        def one(i):
+            q = (own_source + i) % (2 * SIDE)
+            send(
+                answers.at[q, :, cols(j)], returned.at[answer_slot(q), :, cols(j)],
+                ret_send.at[j, q], ret_recv.at[j, answer_slot(q)], source_at(q),
+            )
+
+        loop(1, 2 * SIDE, one)
+        returned[own_expert, :, cols(j)] = answers[own_source, :, cols(j)]
+
+    loop(0, CHUNKS, answer)
+
+    def combine(j):
+        def arrived(k):
+            e = (own_expert + k) % (2 * SIDE)
+            wait(returned.at[e, :, cols(j)], ret_recv.at[j, e])
+
+        loop(1, 2 * SIDE, arrived)
+        rows = returned[:, :, cols(j)].reshape(tokens, size)
+        result = jnp.dot(weigh[...], rows, preferred_element_type=jnp.float32)
+        partial[:, :, :, cols(j)] = result.astype(jnp.bfloat16).reshape(SIDE, SIDE, 16, size)
+
+    def combine_rows(j):
+        combine(j)
+
+        def one(d):
+            r = (y + d) % SIDE
+            send(
+                partial.at[r, :, :, cols(j)], landed.at[y, :, :, cols(j)],
+                c_send.at[j, r], c_recv.at[j, y], peer_row(r),
+            )
+
+        others(one)
+
+    loop(0, last, combine_rows)
+    combine(last)
+
+    def one_last(d):
+        f = (first + d) % SIDE
+        send(
+            partial.at[:, f, :, cols(last)], landed.at[first, :, :, cols(last)],
+            c_send.at[last, f], c_recv.at[last, first], peer_first(f),
+        )
+
+    others(one_last)
+
+    def add_up(own, j, index):
+        block = own.astype(jnp.float32)
+        for d in range(1, SIDE):
+            block = block + landed[(index + d) % SIDE, :, :, cols(j)].astype(jnp.float32)
+        summed[:, :, cols(j)] = block.astype(jnp.bfloat16)
+
+    def gather_rows(j):
+        wait_others(landed.at[0, :, :, cols(j)], y, c_recv.at[j])
+        add_up(partial[y, :, :, cols(j)], j, y)
+
+        def one(d):
+            f = (first + d) % SIDE
+            send(
+                summed.at[f, :, cols(j)], landed_last.at[first, :, cols(j)],
+                d_send.at[j, f], d_recv.at[j, first], peer_first(f),
+            )
+
+        others(one)
+
+    loop(0, last, gather_rows)
+    wait_others(landed.at[0, :, :, cols(last)], first, c_recv.at[last])
+    add_up(partial[:, first, :, cols(last)], last, first)
+
+    def one_row(d):
+        r = (y + d) % SIDE
+        send(
+            summed.at[r, :, cols(last)], landed_last.at[y, :, cols(last)],
+            d_send.at[last, r], d_recv.at[last, y], peer_row(r),
+        )
+
+    others(one_row)
+
+    def finish(j, index):
+        wait_others(landed_last.at[0, :, cols(j)], index, d_recv.at[j])
+        block = summed[index, :, cols(j)].astype(jnp.float32)
+        for d in range(1, SIDE):
+            block = block + landed_last[(index + d) % SIDE, :, cols(j)].astype(jnp.float32)
+        mixed[:, cols(j)] = (attended[:, cols(j)].astype(jnp.float32) + block).astype(jnp.bfloat16)
+
+    loop(0, last, lambda j: finish(j, first))
+    finish(last, y)
+
+    def sent(j, index, other):
+        wait_others(normed.at[:, cols(j)], index, a_send.at[j])
+        wait_others(rows_held.at[0, :, :, cols(j)], other, b_send.at[j])
+        wait_others(partial.at[0, :, :, cols(j)], other, c_send.at[j])
+        wait_others(summed.at[0, :, cols(j)], index, d_send.at[j])
+
+        def one(i):
+            wait(picked.at[0, :, cols(j)], out_send.at[j, (own_expert + i) % (2 * SIDE)])
+            wait(answers.at[0, :, cols(j)], ret_send.at[j, (own_source + i) % (2 * SIDE)])
+
+        loop(1, 2 * SIDE, one)
+
+    loop(0, last, lambda j: sent(j, first, y))
+    sent(last, y, first)
+    wait_others(meta.at[y, first], first, meta_sems.at[0])
+    wait_others(meta.at[y], y, meta_sems.at[2])
+
+
+def mix(normed, attended, ids, probs, gate_up, down):
+    rows, width = normed.shape
+    hidden = down.shape[1]
+    tokens = SIDE * SIDE * rows
+    vmem = pl.BlockSpec(memory_space=pltpu.VMEM)
+    hbm = pl.BlockSpec(memory_space=pl.ANY)
+    sems = pltpu.SemaphoreType.DMA
+    bf16 = jnp.bfloat16
+    return pl.pallas_call(
+        experts_kernel,
+        out_shape=jax.ShapeDtypeStruct((rows, width), bf16),
+        in_specs=[vmem, vmem, vmem, vmem, hbm, hbm],
+        out_specs=vmem,
+        scratch_shapes=[
+            pltpu.VMEM((width, 2 * hidden), bf16),
+            pltpu.VMEM((hidden, width), bf16),
+            pltpu.VMEM((SIDE, SIDE, rows, 256), bf16),
+            pltpu.VMEM((SIDE, SIDE, rows, width), bf16),
+            pltpu.VMEM((2 * SIDE, 32, width), bf16),
+            pltpu.VMEM((2 * SIDE, 32, width), bf16),
+            pltpu.VMEM((tokens, 2 * hidden), jnp.float32),
+            pltpu.VMEM((2 * SIDE, 32, width), bf16),
+            pltpu.VMEM((2 * SIDE, 32, width), bf16),
+            pltpu.VMEM((SIDE, SIDE, rows, width), bf16),
+            pltpu.VMEM((SIDE, SIDE, rows, width), bf16),
+            pltpu.VMEM((SIDE, rows, width), bf16),
+            pltpu.VMEM((SIDE, rows, width), bf16),
+            pltpu.VMEM((tokens, tokens), bf16),
+            pltpu.VMEM((tokens, tokens), bf16),
+            sems((2 * CHUNKS,)),
+            sems((4, SIDE)),
+            sems((CHUNKS, SIDE)),
+            sems((CHUNKS, SIDE)),
+            sems((CHUNKS, SIDE)),
+            sems((CHUNKS, SIDE)),
+            sems((CHUNKS, 2 * SIDE)),
+            sems((CHUNKS, 2 * SIDE)),
+            sems((CHUNKS, 2 * SIDE)),
+            sems((CHUNKS, 2 * SIDE)),
+            sems((CHUNKS, SIDE)),
+            sems((CHUNKS, SIDE)),
+            sems((CHUNKS, SIDE)),
+            sems((CHUNKS, SIDE)),
+        ],
+        compiler_params=pltpu.CompilerParams(
+            collective_id=2, has_side_effects=True, vmem_limit_bytes=58 << 20
+        ),
+        name="experts",
+    )(normed, attended, ids, probs, gate_up, down)
 
 
 def local(
@@ -94,51 +651,8 @@
     head_list = attend_block(
         query, new_key_value, cached_key_rows, cached_value_rows, lengths, q_gain, k_gain
     )
-    gathered = jnp.dot(
-        lax.all_gather(head_list, "ep", axis=0, tiled=True),
-        out_weight,
-        preferred_element_type=jnp.float32,
-    ).astype(jnp.bfloat16)
-    projected = lax.all_to_all(gathered, "ep", split_axis=0, concat_axis=1, tiled=True)
-    attended = (residual.astype(jnp.float32) + projected.astype(jnp.float32)).astype(jnp.bfloat16)
-    stream = attended.astype(jnp.float32)
-    normed = (
-        stream * lax.rsqrt(jnp.mean(stream * stream, axis=-1, keepdims=True) + EPSILON) * moe_gain
-    ).astype(jnp.bfloat16)
-    weights = gate_probs / jnp.sum(gate_probs, axis=-1, keepdims=True)
-    tok_count, top_count = expert_ids.shape
-    width = residual.shape[1]
-    dp_size = lax.axis_size("dp")
-    ep_size = lax.axis_size("ep")
-    owner_count = dp_size * ep_size
-    capacity = max(2, tok_count * top_count * 2 // owner_count)
-    flat_ids = expert_ids.reshape(-1)
-    matches = (flat_ids[:, None] == jnp.arange(owner_count, dtype=jnp.int32)[None, :]).astype(
-        jnp.int32
-    )
-    earlier = jnp.cumsum(matches, axis=0) - matches
-    slots = jnp.sum(earlier * matches, axis=1)
-    targets = flat_ids * capacity + slots
-    placing = (
-        jnp.arange(owner_count * capacity, dtype=jnp.int32)[:, None, None]
-        == targets.reshape(tok_count, top_count)[None]
-    ).astype(jnp.int32)
-    placing = jnp.sum(placing, axis=2).astype(jnp.bfloat16)
-    outgoing = jnp.dot(placing, normed, preferred_element_type=jnp.float32).astype(jnp.bfloat16)
-    outgoing = outgoing.reshape(owner_count, capacity, width)
-    gate_up = expert_gate_up[0]
-    down = expert_down[0]
-    rows = lax.all_to_all(outgoing, ("dp", "ep"), split_axis=0, concat_axis=0, tiled=True)
-    sources, items, row_width = rows.shape
-    result = expert_rows(rows.reshape(sources * items, row_width), gate_up, down)
-    answers = result.reshape(sources, items, row_width)
-    returned = lax.all_to_all(
-        answers.astype(jnp.bfloat16), ("dp", "ep"), split_axis=0, concat_axis=0, tiled=True
-    ).astype(answers.dtype)
-    returned = returned.reshape(owner_count * capacity, width)
-    picked = returned[targets].reshape(tok_count, top_count, width)
-    moe_out = jnp.sum(weights[:, :, None] * picked, axis=1)
-    mixed = (stream + moe_out).astype(jnp.bfloat16)
+    attended, normed = project(head_list, residual, out_weight, moe_gain.reshape(1, -1))
+    mixed = mix(normed, attended, expert_ids, gate_probs, expert_gate_up, expert_down)
     return (attended, mixed)
 
 

time: 202 us -> 117 us (0.58)
  Pallas kernels: 0 us -> 104 us
  waiting for transfers between devices: 87 us -> 0 us
  blocking collectives: 36.4 us -> 0 us
  matrix products: 19.6 us -> 1.52 us
  local copies, waits for them, and re-layouts: 23.5 us -> 5.74 us
  between operations: 14.3 us -> 0.83 us
  starting transfers between devices: 11.1 us -> 0 us
  other arithmetic: 9.83 us -> 5.18 us
    pallas_call x0 -> x2, Pallas kernels: none -> 104 us  [the longest x1 74.6 us: mix(): pl.pallas_call(experts_kernel, out_shape=jax.ShapeDtypeStruct((rows, widt...]
    all_gather x1 -> x0, waiting for transfers between devices: 49.4 us -> none  [local(): lax.all_gather(head_list, 'ep', axis=0, tiled=True)]
    all_to_all x2 -> x0, waiting for transfers between devices: 37.6 us -> none  [the longest x1 30.1 us: local(): lax.all_to_all(answers.astype(jnp.bfloat16), ('dp', 'ep'), split_axis=0,...]
    all_to_all x1 -> x0, blocking collectives: 36.4 us -> none  [local(): lax.all_to_all(outgoing, ('dp', 'ep'), split_axis=0, concat_axis=0, tiled...]
    dot_general x4 -> x0, matrix products: 18 us -> none  [the longest x1 7.02 us: expert_rows(): both = jnp.dot(rows, gate_up, preferred_element_type=jnp.float32)]
    reshape x3 -> x0, local copies, waits for them, and re-layouts: 12.9 us -> none  [the longest x1 4.39 us: local(): outgoing = outgoing.reshape(owner_count, capacity, width)]
    all_to_all x2 -> x0, starting transfers between devices: 11 us -> none  [the longest x1 5.74 us: local(): lax.all_to_all(answers.astype(jnp.bfloat16), ('dp', 'ep'), split_axis=0,...]
    gather x1 -> x0, local copies, waits for them, and re-layouts: 5.63 us -> none  [local(): picked = returned[targets].reshape(tok_count, top_count, width)]
  transfers between devices with their start and end apart: 3 -> 0, of which waited for: 3 -> 0; matrix products, arithmetic and copies ran while one was open for 0% -> 0% of each run, Pallas kernels for 0% -> 0%
where the time goes in v1:
time: 117 us
  Pallas kernels  104 us (89%)
  local copies, waits for them, and re-layouts  5.74 us (5%)
  other arithmetic  5.18 us (4%)
  matrix products  1.52 us (1%)
    pallas_call x1, Pallas kernels, mix(): pl.pallas_call(experts_kernel, out_shape=jax.ShapeDtypeStruct((rows, widt...  74.6 us
    pallas_call x1, Pallas kernels, project(): pl.pallas_call(project_kernel, out_shape=[jax.ShapeDtypeStruct((rows, wid...  29.4 us
    unnamed x28, local copies, waits for them, and re-layouts  5.74 us

profile of v1, /device:TPU:1, one launch (start us, length us, event | category | flops | bytes accessed | tf_op | source)
XLA Modules:
  0.0 117.2 jit_solution(11160610455465932057)
XLA Ops:
  0.6 0.0 copy-start
  0.6 0.0 copy-start.9
  0.7 0.9 slice_convert_fusion
  1.6 0.1 multiply_reduce_fusion.1
  1.7 0.7 multiply_multiply_fusion.1
  2.4 0.7 convert_element_type.51
  3.1 0.1 multiply_cosine_fusion
  3.2 0.1 subtract_convert_fusion.1
  3.3 0.1 maximum_bitcast_fusion
  3.4 0.9 convert_bitcast_fusion
  4.3 0.1 copy.24
  4.4 0.2 multiply_reduce_fusion
  4.6 0.8 multiply_multiply_fusion
  5.4 0.1 subtract_convert_fusion
  5.5 0.0 copy-start.10
  5.6 0.2 fusion.23
  5.8 0.0 copy-done.9
  5.8 0.1 iota_compare_fusion
  5.9 0.0 copy-done
  5.9 0.8 fusion.30
  6.7 0.3 fusion.18
  7.1 0.1 copy-done.10
  7.1 0.0 copy-start.1
  7.1 0.0 copy-start.5
  7.1 0.0 copy-start.6
  7.1 0.0 copy-start.7
  7.1 0.0 copy-start.8
  7.2 0.5 fusion.15
  7.6 0.1 copy.47
  7.7 0.7 copy-done.1
  8.4 0.0 copy-done.5
  8.4 0.0 copy-done.6
  8.4 29.4 %project.1 = (bf16[16,4096]{1,0:T(8,128)(2,1)S(1)}, bf16[16,4096]{1,0:T(8,128)(2,1)S(1)}) custom-call(bf16[16,4096]{1,0:T(8,128)(2,1)S(1)} %bitcast.40, bf16[16,4096]{1,0:T(8,128)(2,1)S(1)} %copy-done.5, bf16[4096,128]{1,0:T(8,128)(2,1)S(1)} %copy-done.1, f32[1,4096]{1,0:T(1,128)S(1)} %bitcast.41), custom_call_target="tpu_custom_call" | custom-call | tf_op jit(solution)/shard_map/project/pallas_call | solution.py:237
  37.8 0.0 copy-start.2
  37.8 0.6 copy-done.2
  38.4 0.0 copy-start.4
  38.4 0.7 copy-done.4
  39.1 0.0 copy-done.7
  39.1 0.7 copy.18.ids
  39.7 0.0 copy-done.8
  39.7 0.7 copy.19.probs
  40.4 0.0 copy-start.3
  40.4 74.6 %experts.1 = bf16[16,4096]{1,0:T(8,128)(2,1)} custom-call(bf16[16,4096]{1,0:T(8,128)(2,1)} %copy-done.4, bf16[16,4096]{1,0:T(8,128)(2,1)} %copy-done.2, s32[16,8]{1,0:T(8,128)} %copy.18.ids, f32[16,8]{1,0:T(8,128)} %copy.19.probs, bf16[1,4096,1536]{2,1,0:T(8,128)(2,1)} %gate_up.1, bf16[1,768,4096]{2,1,0:T(8,128)(2,1)} %down.1), custom_call_target="tpu_custom_call" | custom-call | tf_op jit(solution)/shard_map/experts/pallas_call | solution.py:592
  115.0 0.0 copy-done.3
  115.0 0.7 copy.50
  115.6 1.6 %copy.51 = bf16[16,4096]{1,0:T(8,128)(2,1)} copy(bf16[16,4096]{1,0:T(8,128)(2,1)} %experts.1) | data formatting | bytes 262144
  (5 shorter events, 0.1 us)
Async XLA Ops:
  0.6 5.3 %copy-start = (bf16[16,256,256]{2,1,0:T(8,128)(2,1)S(1)}, bf16[16,256,256]{2,1,0:T(8,128)(2,1)}, u32[]{:S(2)}) copy-start(bf16[16,256,256]{2,1,0:T(8,128)(2,1)} %param.17) | copy-start | bytes 6291460
  0.6 5.2 %copy-start.9 = (s32[16]{0:T(128)S(1)}, s32[16]{0:T(128)}, u32[]{:S(2)}) copy-start(s32[16]{0:T(128)} %param.19) | copy-start | bytes 196
  5.5 1.6 %copy-start.10 = (bf16[16,256,256]{2,1,0:T(8,128)(2,1)S(1)}, bf16[16,256,256]{2,1,0:T(8,128)(2,1)}, u32[]{:S(2)}) copy-start(bf16[16,256,256]{2,1,0:T(8,128)(2,1)} %param.18) | copy-start | bytes 6291460
  7.1 1.2 %copy-start.1 = (bf16[4096,128]{1,0:T(8,128)(2,1)S(1)}, bf16[4096,128]{1,0:T(8,128)(2,1)}, u32[]{:S(2)}) copy-start(bf16[4096,128]{1,0:T(8,128)(2,1)} %weight.1) | copy-start | bytes 3145732
  7.1 1.2 %copy-start.5 = (bf16[16,4096]{1,0:T(8,128)(2,1)S(1)}, bf16[16,4096]{1,0:T(8,128)(2,1)}, u32[]{:S(2)}) copy-start(bf16[16,4096]{1,0:T(8,128)(2,1)} %residual.1) | copy-start | bytes 393220
  7.1 1.2 %copy-start.6 = (f32[4096]{0:T(1024)S(1)}, f32[4096]{0:T(1024)}, u32[]{:S(2)}) copy-start(f32[4096]{0:T(1024)} %param.23) | copy-start | bytes 49156
  7.1 31.9 %copy-start.7 = (s32[16,8]{0,1:T(8,128)S(1)}, s32[16,8]{0,1:T(8,128)}, u32[]{:S(2)}) copy-start(s32[16,8]{0,1:T(8,128)} %param.24) | copy-start | bytes 1540
  7.1 32.6 %copy-start.8 = (f32[16,8]{0,1:T(8,128)S(1)}, f32[16,8]{0,1:T(8,128)}, u32[]{:S(2)}) copy-start(f32[16,8]{0,1:T(8,128)} %param.25) | copy-start | bytes 1540
  37.8 0.7 copy-start.2
  38.4 0.7 copy-start.4
  40.4 74.6 %copy-start.3 = (bf16[16,4096]{1,0:T(8,128)(2,1)S(1)}, bf16[16,4096]{1,0:T(8,128)(2,1)}, u32[]{:S(2)}) copy-start(bf16[16,4096]{1,0:T(8,128)(2,1)} %copy-done.2) | copy-start | bytes 393220

commit v2 on v0

v2 whole, which is shorter than its diff:
```python
import math

import jax
import jax.numpy as jnp
from jax import lax
from jax.experimental import pallas as pl
from jax.experimental.pallas import tpu as pltpu
from jax.sharding import PartitionSpec as P

EPSILON = 1e-06
THETA = 1000000.0


MESH = pl.DeviceIdType.MESH
SIDE = 4
PLANE = 2 * SIDE * SIDE
GROUPS = ((0, 1280), (1280, 1536), (2816, 1280))
PARTS = (((0, 384), (0, 384), (0, 384)), ((384, 256), (384, 384), (384, 256)))


def place():
    y = lax.axis_index("dp")
    e = lax.axis_index("ep")
    return (e // 2) % SIDE, y, e // (2 * SIDE), e % 2


def device(x, y, z, core):
    return (y, (z * SIDE + x) * 2 + core)


def signal(target):
    pl.semaphore_signal(
        pltpu.get_barrier_semaphore(), inc=1, device_id=target, device_id_type=MESH
    )


def send(source, target, send_sem, recv_sem, where):
    pltpu.make_async_remote_copy(
        src_ref=source,
        dst_ref=target,
        send_sem=send_sem,
        recv_sem=recv_sem,
        device_id=where,
        device_id_type=MESH,
    ).start()


def wait(ref, sem):
    pltpu.make_async_copy(ref, ref, sem).wait()


def loop(first, last, body):
    def step(i, carry):
        body(i)
        return carry

    lax.fori_loop(first, last, step, 0)


def near_first(i):
    return 1 + 2 * i - 3 * (i // 2)


def route(ids, probs):
    top, count = ids.shape
    experts = 128
    weights = probs / jnp.sum(probs, axis=0, keepdims=True)
    label = iota((experts, count), 0)
    named = jnp.zeros((experts, count), jnp.float32)
    value = jnp.zeros((experts, count), jnp.float32)
    for k in range(top):
        match = ids[k : k + 1] == label
        named = named + jnp.where(match, 1.0, 0.0)
        value = value + jnp.where(match, weights[k : k + 1], 0.0)
    before = jnp.where(iota((count, count), 0) < iota((count, count), 1), 1.0, 0.0)
    earlier = jnp.dot(named, before, preferred_element_type=jnp.float32)
    again = earlier > 0.5
    both = jnp.concatenate(
        [jnp.where(again, 0.0, value), jnp.where(again, value, 0.0)], axis=0
    )
    return both.T.astype(jnp.bfloat16)


def turned(rows, cosines, sines, gain):
    mean_square = jnp.mean(rows * rows, axis=-1, keepdims=True)
    scaled = rows * lax.rsqrt(mean_square + EPSILON) * gain
    return (scaled * cosines + pltpu.roll(scaled, 64, 1) * sines).astype(jnp.bfloat16)


def halves(rows):
    width = rows.shape[1] // 2
    parts = rows.reshape(PLANE, 8, 2 * width)
    return jnp.concatenate([parts[:, :, :width], parts[:, :, width:]], axis=1).astype(jnp.bfloat16)


def iota(shape, dim):
    return lax.broadcasted_iota(jnp.int32, shape, dim)


def shifted(value, by, size):
    return (value >> by) & (size - 1)


def spot(axis, a, b, f):
    return ((f, a, b), (b, f, a), (b, a, f))[axis]


def ordered(axis, p, f, slot):
    x, y, z = spot(axis, shifted(p, 3, SIDE), shifted(p, 1, SIDE), f)
    return ((y * SIDE + z) * SIDE + x) * 4 + (p & 1) * 2 + slot


def ones_where(condition):
    return jnp.where(condition, 1.0, 0.0).astype(jnp.bfloat16)


def kernel(
    residual_in, query_in, new_in, keys_in, values_in, lengths, q_gain, k_gain, weight, moe_gain, ids, probs,
    gate_up, down, attended, mixed,
    query, keys, values, residual, scores, products_pv, heads, columns_held, blocks, products, projected,
    normed, gate_up_held, down_held, meta, shared, picked, received, total, answers, returned,
    partial, landed, choose, weigh, gather, spread,
    cache_sems, head_weight_sems, first_send, first_recv, second_send, second_recv, back_send, back_recv,
    weight_sems, meta_send, meta_recv, share_send, share_recv, out_send, out_recv,
    ret_send, ret_recv, sum_send, sum_recv,
):
    x, y, z, core = place()
    along = (x, y, z)
    across = ((y, z), (z, x), (y, x))
    axes = range(3)
    index = [(a * SIDE + b) * 2 + core for a, b in across]

    def on_line(axis, f):
        return device(*[f if i == axis else along[i] for i in axes], core)

    def in_plane(axis, p):
        return device(*spot(axis, p // (2 * SIDE), (p // 2) % SIDE, along[axis]), p % 2)

    def partner(axis, i):
        step = (13 * i) % PLANE
        a, b = across[axis]
        return (((a + step // (2 * SIDE)) % SIDE) * SIDE + (b + step // 2) % SIDE) * 2 + (core + step) % 2

    def each_partner(body):
        def one(i):
            for axis in axes:
                body(axis, partner(axis, i))

        loop(1, PLANE, one)

    def columns(axis):
        return pl.ds(*GROUPS[axis])

    def lanes(part, axis):
        start, size = PARTS[part][axis]
        return pl.ds(GROUPS[axis][0] // 2 + start, size)

    def both_columns(part, axis):
        start, size = PARTS[part][axis]
        base, width = GROUPS[axis]
        return pl.ds(base + start, size), pl.ds(base + width // 2 + start, size)

    loads = [
        pltpu.make_async_copy(source, target, cache_sems.at[i])
        for i, (source, target) in enumerate(
            ((query_in, query), (keys_in, keys), (values_in, values), (residual_in, residual))
        )
    ]
    for load in loads:
        load.start()
    half = pl.ds(pl.multiple_of(core * 128, 128), 128)
    own_weight = pltpu.make_async_copy(weight, columns_held.at[:, half], head_weight_sems.at[0])
    own_weight.start()
    each_partner(lambda axis, p: signal(in_plane(axis, p)))
    rows_of = [pl.ds(*group) for group in GROUPS]
    fetches = [
        pltpu.make_async_copy(gate_up.at[0, rows], gate_up_held.at[rows], weight_sems.at[i])
        for i, rows in enumerate(rows_of)
    ] + [
        pltpu.make_async_copy(down.at[0, :, rows], down_held.at[:, rows], weight_sems.at[3 + i])
        for i, rows in enumerate(rows_of)
    ]
    for fetch in fetches:
        fetch.start()
    own_meta = route(ids[...], probs[...])
    for axis in axes:
        meta[axis, along[axis]] = own_meta

    tokens, slots, group = 16, keys.shape[1], 16
    pairs = tokens * group
    nt = (((1,), (1,)), ((), ()))

    def exact(left, right, dims=(((1,), (0,)), ((), ()))):
        return lax.dot_general(left, right, dims, preferred_element_type=jnp.float32)

    count = jnp.broadcast_to(lengths[...].astype(jnp.float32), (128, tokens)).astype(jnp.bfloat16)
    same_token = ones_where(iota((pairs, tokens), 0) >> 4 == iota((pairs, tokens), 1))
    eye = ones_where(iota((tokens, tokens), 0) == iota((tokens, tokens), 1))
    position = exact(eye, count, nt)
    lane = iota((tokens, 128), 1)
    freqs = jnp.exp((lane & 63).astype(jnp.float32) * (-2.0 * math.log(THETA) / 128))
    angles = position * freqs
    cosines = jnp.cos(angles)
    sines = jnp.where(lane < 64, -1.0, 1.0) * jnp.sin(angles)
    row, col = iota((pairs, pairs), 0), iota((pairs, pairs), 1)
    swap = ones_where(((row >> 4) == (col & 15)) & ((row & 15) == (col >> 4)))
    live = iota((pairs, slots), 1) < jnp.concatenate(
        [exact(same_token, count, nt)] * (slots // 128), axis=1
    ).astype(jnp.int32)
    scale = 1.0 / math.sqrt(128)
    many_cosines = jnp.concatenate([cosines] * group, axis=0)
    many_sines = jnp.concatenate([sines] * group, axis=0)
    loads[0].wait()
    queries, own_scores = [], []
    for kv in range(2):
        stack = jnp.concatenate(
            [query[:, (kv * group + h) * 128 : (kv * group + h + 1) * 128] for h in range(group)], axis=0
        ).astype(jnp.float32)
        rotated = exact(swap, turned(stack, many_cosines, many_sines, q_gain[...]))
        new_key = turned(
            new_in[:, kv * 128 : kv * 128 + 128].astype(jnp.float32), cosines, sines, k_gain[...]
        )
        own = jnp.sum(rotated * exact(same_token, new_key), axis=-1, keepdims=True) * scale
        queries.append(rotated.astype(jnp.bfloat16))
        own_scores.append(own)
    loads[1].wait()
    for kv in range(2):
        lanes_of = slice(kv * 128, kv * 128 + 128)
        for t in range(tokens):
            scores[kv, t * group : (t + 1) * group] = exact(
                queries[kv][t * group : (t + 1) * group], keys[t, :, lanes_of], nt
            )
    loads[2].wait()

    def attend(kv):
        lanes_of = slice(kv * 128, kv * 128 + 128)
        own = own_scores[kv]
        masked = jnp.where(live, scores[kv] * scale, -jnp.inf)
        highest = jnp.maximum(jnp.max(masked, axis=-1, keepdims=True), own)
        expos = jnp.exp(masked - highest)
        own_expo = jnp.exp(own - highest)
        sums = jnp.sum(expos, axis=-1, keepdims=True) + own_expo
        probs_of = (expos / sums).astype(jnp.bfloat16)
        own_prob = (own_expo / sums).astype(jnp.bfloat16).astype(jnp.float32)
        for t in range(tokens):
            products_pv[t * group : (t + 1) * group] = exact(
                probs_of[t * group : (t + 1) * group], values[t, :, lanes_of]
            )
        new_value = exact(same_token, new_in[:, 256 + kv * 128 : 384 + kv * 128])
        result = (products_pv[...] + own_prob * new_value).astype(jnp.bfloat16)
        result = exact(swap, result).astype(jnp.bfloat16)
        for h in range(group):
            heads[:, (kv * group + h) * 128 : (kv * group + h + 1) * 128] = result[
                h * tokens : (h + 1) * tokens
            ]

    first = x * (1 - core) + z * core
    second = z * (1 - core) + x * core

    def at(f, s):
        return device(f * (1 - core) + s * core, y, s * (1 - core) + f * core, core)

    width = heads.shape[1]
    wide = width // 2

    def side(kv):
        return pl.ds(kv * wide, wide)

    def start_first(kv):
        def one(i):
            f = (first + near_first(i)) % SIDE
            send(
                heads.at[:, side(kv)], blocks.at[second, first, :, side(kv)],
                first_send.at[kv, f], first_recv.at[kv, first], at(f, second),
            )

        loop(0, SIDE - 1, one)

    def start_second(kv, f, source):
        def one(i):
            s = (second + near_first(i)) % SIDE
            send(
                source, blocks.at[second, f, :, side(kv)], second_send.at[kv, s, f],
                second_recv.at[kv, second, f], at(first, s),
            )

        loop(0, SIDE - 1, one)

    sibling = device(x, y, z, 1 - core)
    attend(0)
    pl.semaphore_wait(pltpu.get_barrier_semaphore(), 3 * (PLANE - 1))
    start_first(0)
    start_second(0, first, heads.at[:, side(0)])
    attend(1)
    start_first(1)
    start_second(1, first, heads.at[:, side(1)])
    send(weight, columns_held.at[:, half], head_weight_sems.at[1], head_weight_sems.at[2], sibling)

    def to_line(axis, body):
        def one(i):
            body((along[axis] + near_first(i)) % SIDE)

        loop(0, SIDE - 1, one)

    for axis in axes:
        own = along[axis]
        to_line(axis, lambda f: send(
            meta.at[axis, own], meta.at[axis, own], meta_send.at[axis, f], meta_recv.at[axis, own],
            on_line(axis, f),
        ))
    blocks[second, first] = heads[...]
    for kv in range(2):
        def pass_on(i):
            f = (first + near_first(i)) % SIDE
            wait(blocks.at[second, f, :, side(kv)], first_recv.at[kv, f])
            start_second(kv, f, blocks.at[second, f, :, side(kv)])

        loop(0, SIDE - 1, pass_on)
    own_weight.wait()
    wait(weight, head_weight_sems.at[2])
    mine = pl.ds(pl.multiple_of((z * SIDE + x) * 256, 256), 256)

    def project(s):
        rows = blocks[s].reshape(SIDE * tokens, width)
        products[s] = exact(rows, columns_held[...]).astype(jnp.bfloat16).reshape(SIDE, tokens, 256)

    def back(f, s):
        send(
            products.at[s, f], projected.at[:, mine], back_send.at[s, f],
            back_recv.at[second, first], at(f, s),
        )

    project(second)
    projected[:, mine] = products[second, first]
    loop(0, SIDE - 1, lambda i: back((first + near_first(i)) % SIDE, second))

    for axis in axes:
        q = iota((1, 512), 1)
        target = ordered(axis, q >> 4, shifted(q, 1, SIDE), q & 1) + shifted(q, 3, 2) * 256
        gather[axis] = ones_where(iota((512, 512), 0) == target)
        q = iota((256, 1), 0)
        target = ordered(axis, q >> 3, shifted(q, 1, SIDE), q & 1)
        spread[axis] = ones_where(iota((256, 256), 1) == target)

    for axis in axes:
        to_line(axis, lambda f: wait(meta.at[axis, 0], meta_recv.at[axis, f]))
        known = meta[axis].reshape(SIDE * 16, 256)
        present = ones_where(known.astype(jnp.float32) > 0.0)

        def expert(p):
            ex, ey, ez = spot(axis, shifted(p, 3, SIDE), shifted(p, 1, SIDE), along[axis])
            return (ey * SIDE + ez) * (2 * SIDE) + ex * 2 + (p & 1)

        q = iota((256, 1), 0)
        wanted = ones_where(iota((256, 256), 1) == (q & 1) * 128 + expert(q >> 3))
        chosen = lax.dot_general(wanted, present, nt, preferred_element_type=jnp.float32)
        same = shifted(q, 1, SIDE) == iota((1, SIDE * 16), 1) >> 4
        choose[axis] = jnp.where(same, chosen, 0.0).astype(jnp.bfloat16)
        q = iota((512, 1), 0)
        wanted = ones_where(iota((512, 256), 1) == (q & 1) * 128 + expert(q >> 4))
        scaled = lax.dot_general(known, wanted, nt, preferred_element_type=jnp.float32)
        q = iota((1, 512), 1)
        scaled = jnp.where(iota((SIDE * 16, 1), 0) >> 4 == shifted(q, 1, SIDE), scaled, 0.0)
        upper = shifted(q, 3, 2) == 0
        weigh[axis] = jnp.concatenate(
            [jnp.where(upper, scaled, 0.0), jnp.where(upper, 0.0, scaled)], axis=0
        ).astype(jnp.bfloat16)

    def other_group(i):
        s = (second + near_first(i)) % SIDE

        def arrived(f):
            for kv in range(2):
                wait(blocks.at[s, f, :, side(kv)], second_recv.at[kv, s, f])

        loop(0, SIDE, arrived)
        project(s)
        loop(0, SIDE, lambda f: back(f, s))

    loop(0, SIDE - 1, other_group)

    def others_in_plane(body):
        def one(i):
            other = (second * SIDE + first + i) % (SIDE * SIDE)
            body(other % SIDE, other // SIDE)

        loop(1, SIDE * SIDE, one)

    others_in_plane(lambda f, s: wait(products.at[s, f], back_recv.at[s, f]))
    loads[3].wait()
    added = residual[...].astype(jnp.float32) + projected[...].astype(jnp.float32)
    rounded = added.astype(jnp.bfloat16)
    attended[...] = rounded
    stream = rounded.astype(jnp.float32)
    level = lax.rsqrt(jnp.mean(stream * stream, axis=-1, keepdims=True) + EPSILON)
    normed[...] = (stream * level * moe_gain[...]).astype(jnp.bfloat16)
    for axis in axes:
        own = along[axis]
        to_line(axis, lambda f: send(
            normed.at[:, columns(axis)], shared.at[own, :, columns(axis)],
            share_send.at[axis, f], share_recv.at[axis, own], on_line(axis, f),
        ))
        shared[along[axis], :, columns(axis)] = normed[:, columns(axis)]

    for axis in axes:
        to_line(axis, lambda f: wait(shared.at[0, :, columns(axis)], share_recv.at[axis, f]))
        rows = shared[:, :, columns(axis)].reshape(SIDE * 16, GROUPS[axis][1])
        result = jnp.dot(choose[axis], rows, preferred_element_type=jnp.float32)
        base, width = GROUPS[axis]
        picked[:, :, pl.ds(base // 2, width // 2)] = halves(result)
    for part in range(len(PARTS)):
        each_partner(lambda axis, p: send(
            picked.at[p, :, lanes(part, axis)], received.at[index[axis], :, lanes(part, axis)],
            out_send.at[part, axis], out_recv.at[part, axis], in_plane(axis, p),
        ))
    for axis in axes:
        base, width = GROUPS[axis]
        whole = pl.ds(base // 2, width // 2)
        received[index[axis], :, whole] = picked[index[axis], :, whole]

    hidden_size = down.shape[1]
    many = pl.ds(0, PLANE - 1)
    for part in range(len(PARTS)):
        for axis in axes:
            wait(received.at[many, :, lanes(part, axis)], out_recv.at[part, axis])
            if part == 0:
                fetches[axis].wait()
            size = PARTS[part][axis][1]
            messages = received[:, :, lanes(part, axis)].reshape(PLANE * 16, size)
            rows = jnp.dot(gather[axis], messages, preferred_element_type=jnp.float32)
            rows = rows.astype(jnp.bfloat16)
            upper, lower = both_columns(part, axis)

            def step(n):
                piece = pl.ds(pl.multiple_of(n * 512, 512), 512)
                product = jnp.dot(
                    rows[:256], gate_up_held[upper, piece], preferred_element_type=jnp.float32
                ) + jnp.dot(
                    rows[256:], gate_up_held[lower, piece], preferred_element_type=jnp.float32
                )
                if part == 0 and axis == 0:
                    total[:, piece] = product
                else:
                    total[:, piece] += product

            loop(0, 2 * hidden_size // 512, step)

    gate = total[:, :hidden_size]
    hidden = (gate / (1.0 + jnp.exp(-gate)) * total[:, hidden_size:]).astype(jnp.bfloat16)
    for axis in axes:
        fetches[3 + axis].wait()
    hiddens = [
        jnp.dot(spread[axis], hidden, preferred_element_type=jnp.float32).astype(jnp.bfloat16)
        for axis in axes
    ]
    for part in range(len(PARTS)):
        for axis in axes:
            upper, lower = both_columns(part, axis)
            result = [
                jnp.dot(hiddens[axis], down_held[:, cols], preferred_element_type=jnp.float32)
                for cols in (upper, lower)
            ]
            answers[:, :, lanes(part, axis)] = halves(jnp.concatenate(result, axis=1))
        each_partner(lambda axis, p: send(
            answers.at[p, :, lanes(part, axis)], returned.at[index[axis], :, lanes(part, axis)],
            ret_send.at[part, axis], ret_recv.at[part, axis], in_plane(axis, p),
        ))
        for axis in axes:
            returned[index[axis], :, lanes(part, axis)] = answers[index[axis], :, lanes(part, axis)]

    for part in range(len(PARTS)):
        for axis in axes:
            wait(returned.at[many, :, lanes(part, axis)], ret_recv.at[part, axis])
            size = PARTS[part][axis][1]
            messages = returned[:, :, lanes(part, axis)].reshape(PLANE * 16, size)
            result = jnp.dot(weigh[axis], messages, preferred_element_type=jnp.float32)
            result = result.astype(jnp.bfloat16).reshape(2, SIDE, 16, size)
            upper, lower = both_columns(part, axis)
            partial[:, :, upper] = result[0]
            partial[:, :, lower] = result[1]
            if part == len(PARTS) - 1:
                own = along[axis]
                to_line(axis, lambda f: send(
                    partial.at[f, :, columns(axis)], landed.at[own, :, columns(axis)],
                    sum_send.at[axis, f], sum_recv.at[axis, own], on_line(axis, f),
                ))
    for axis in axes:
        to_line(axis, lambda f: wait(landed.at[0, :, columns(axis)], sum_recv.at[axis, f]))
        own = along[axis]
        block = partial[own, :, columns(axis)].astype(jnp.float32)
        for d in range(1, SIDE):
            block = block + landed[(own + d) % SIDE, :, columns(axis)].astype(jnp.float32)
        block = block + attended[:, columns(axis)].astype(jnp.float32)
        mixed[:, columns(axis)] = block.astype(jnp.bfloat16)

    wait(weight, head_weight_sems.at[1])
    for kv in range(2):
        def finish_first(i):
            f = (first + 1 + i) % SIDE
            s = (second + 1 + i) % SIDE
            wait(heads.at[:, side(kv)], first_send.at[kv, f])
            loop(0, SIDE, lambda g: wait(heads.at[:, side(kv)], second_send.at[kv, s, g]))

        loop(0, SIDE - 1, finish_first)
    others_in_plane(lambda f, s: wait(products.at[s, f], back_send.at[s, f]))
    for axis in axes:
        to_line(axis, lambda f: wait(meta.at[axis, 0], meta_send.at[axis, f]))
        to_line(axis, lambda f: wait(landed.at[0, :, columns(axis)], share_send.at[axis, f]))
        to_line(axis, lambda f: wait(landed.at[0, :, columns(axis)], sum_send.at[axis, f]))
        for part in range(len(PARTS)):
            wait(picked.at[many, :, lanes(part, axis)], out_send.at[part, axis])
            wait(answers.at[many, :, lanes(part, axis)], ret_send.at[part, axis])


def local(
    residual,
    query,
    new_key_value,
    cached_key_rows,
    cached_value_rows,
    lengths,
    q_gain,
    k_gain,
    out_weight,
    moe_gain,
    expert_ids,
    gate_probs,
    expert_gate_up,
    expert_down,
):
    rows, width = residual.shape
    hidden = expert_down.shape[1]
    slots = cached_key_rows.shape[1]
    vmem = pl.BlockSpec(memory_space=pltpu.VMEM)
    hbm = pl.BlockSpec(memory_space=pl.ANY)
    sems = pltpu.SemaphoreType.DMA
    bf16 = jnp.bfloat16
    own = pltpu.VMEM((rows, width), bf16)
    caches = pltpu.VMEM(cached_key_rows.shape, bf16)
    messages = pltpu.VMEM((PLANE, 16, width // 2), bf16)
    lines = pltpu.VMEM((SIDE, rows, width), bf16)
    parts = len(PARTS)
    attended, mixed = pl.pallas_call(
        kernel,
        out_shape=[jax.ShapeDtypeStruct((rows, width), bf16)] * 2,
        in_specs=[hbm, hbm, vmem, hbm, hbm, vmem, vmem, vmem, hbm, vmem, vmem, vmem, hbm, hbm],
        out_specs=[vmem, vmem],
        scratch_shapes=[
            own,
            caches,
            caches,
            own,
            pltpu.VMEM((2, 256, slots), jnp.float32),
            pltpu.VMEM((256, 128), jnp.float32),
            own,
            pltpu.VMEM((width, 256), bf16),
            pltpu.VMEM((SIDE, SIDE, rows, width), bf16),
            pltpu.VMEM((SIDE, SIDE, rows, 256), bf16),
            own,
            own,
            pltpu.VMEM((width, 2 * hidden), bf16),
            pltpu.VMEM((hidden, width), bf16),
            pltpu.VMEM((3, SIDE, rows, 256), bf16),
            lines,
            messages,
            messages,
            pltpu.VMEM((256, 2 * hidden), jnp.float32),
            messages,
            messages,
            lines,
            lines,
            pltpu.VMEM((3, 256, SIDE * rows), bf16),
            pltpu.VMEM((3, 2 * SIDE * rows, 512), bf16),
            pltpu.VMEM((3, 512, 512), bf16),
            pltpu.VMEM((3, 256, 256), bf16),
            sems((4,)),
            sems((3,)),
            sems((2, SIDE)),
            sems((2, SIDE)),
            sems((2, SIDE, SIDE)),
            sems((2, SIDE, SIDE)),
            sems((SIDE, SIDE)),
            sems((SIDE, SIDE)),
            sems((6,)),
            sems((3, SIDE)),
            sems((3, SIDE)),
            sems((3, SIDE)),
            sems((3, SIDE)),
            sems((parts, 3)),
            sems((parts, 3)),
            sems((parts, 3)),
            sems((parts, 3)),
            sems((3, SIDE)),
            sems((3, SIDE)),
        ],
        compiler_params=pltpu.CompilerParams(
            collective_id=1, has_side_effects=True, vmem_limit_bytes=60 << 20
        ),
        name="layer",
    )(
        residual, query, new_key_value.reshape(rows, 512), cached_key_rows, cached_value_rows,
        lengths.reshape(1, rows), q_gain.reshape(1, 128), k_gain.reshape(1, 128), out_weight,
        moe_gain.reshape(1, width), expert_ids.T, gate_probs.T, expert_gate_up, expert_down,
    )
    return (attended, mixed)


def solution(mesh):
    return jax.shard_map(
        local,
        mesh=mesh,
        in_specs=(
            P(("dp", "ep"), None),
            P(("dp", "ep"), None),
            P(("dp", "ep"), None, None),
            P(("dp", "ep"), None, None),
            P(("dp", "ep"), None, None),
            P(("dp", "ep")),
            P(),
            P(),
            P(None, "ep"),
            P(),
            P(("dp", "ep"), None),
            P(("dp", "ep"), None),
            P(("dp", "ep"), None, None),
            P(("dp", "ep"), None, None),
        ),
        out_specs=(P(("dp", "ep"), None), P(("dp", "ep"), None)),
        check_vma=False,
    )
```

time: 202 us -> 98.3 us (0.49)
  Pallas kernels: 0 us -> 92.9 us
  waiting for transfers between devices: 87 us -> 0 us
  blocking collectives: 36.4 us -> 0 us
  matrix products: 19.6 us -> 0 us
  local copies, waits for them, and re-layouts: 23.5 us -> 4.46 us
  between operations: 14.3 us -> 0.64 us
  starting transfers between devices: 11.1 us -> 0 us
  other arithmetic: 9.83 us -> 0 us
    pallas_call x0 -> x1, Pallas kernels: none -> 92.9 us  [local(): pl.pallas_call(kernel, out_shape=[jax.ShapeDtypeStruct((rows, width), bf1...]
    all_gather x1 -> x0, waiting for transfers between devices: 49.4 us -> none  [local(): lax.all_gather(head_list, 'ep', axis=0, tiled=True)]
    all_to_all x2 -> x0, waiting for transfers between devices: 37.6 us -> none  [the longest x1 30.1 us: local(): lax.all_to_all(answers.astype(jnp.bfloat16), ('dp', 'ep'), split_axis=0,...]
    all_to_all x1 -> x0, blocking collectives: 36.4 us -> none  [local(): lax.all_to_all(outgoing, ('dp', 'ep'), split_axis=0, concat_axis=0, tiled...]
    dot_general x7 -> x0, matrix products: 19.6 us -> none  [the longest x1 7.02 us: expert_rows(): both = jnp.dot(rows, gate_up, preferred_element_type=jnp.float32)]
    reshape x3 -> x0, local copies, waits for them, and re-layouts: 12.9 us -> none  [the longest x1 4.39 us: local(): outgoing = outgoing.reshape(owner_count, capacity, width)]
    all_to_all x2 -> x0, starting transfers between devices: 11 us -> none  [the longest x1 5.74 us: local(): lax.all_to_all(answers.astype(jnp.bfloat16), ('dp', 'ep'), split_axis=0,...]
    gather x1 -> x0, local copies, waits for them, and re-layouts: 5.63 us -> none  [local(): picked = returned[targets].reshape(tok_count, top_count, width)]
  transfers between devices with their start and end apart: 3 -> 0, of which waited for: 3 -> 0; matrix products, arithmetic and copies ran while one was open for 0% -> 0% of each run, Pallas kernels for 0% -> 0%
where the time goes in v2:
time: 98.3 us; the launch traced here: 98 us
  Pallas kernels  92.9 us (95%)
  local copies, waits for them, and re-layouts  4.46 us (5%)
    pallas_call x1, Pallas kernels, local(): pl.pallas_call(kernel, out_shape=[jax.ShapeDtypeStruct((rows, width), bf1...  92.9 us
    unnamed x3, local copies, waits for them, and re-layouts  4.46 us

profile of v2, /device:TPU:1, one launch (start us, length us, event | category | flops | bytes accessed | tf_op | source)
XLA Modules:
  0.0 98.0 jit_solution(6958626265893223475)
XLA Ops:
  0.6 1.3 %copy.16 = bf16[2,8,2,256]{3,1,2,0:T(8,128)(2,1)} copy(bf16[2,8,2,256]{3,2,1,0:T(2,128)(2,1)} %bitcast.10) | data formatting | bytes 32768
  2.0 92.9 %layer.1 = (bf16[16,4096]{1,0:T(8,128)(2,1)}, bf16[16,4096]{1,0:T(8,128)(2,1)}) custom-call(bf16[16,4096]{1,0:T(8,128)(2,1)} %residual_in.1, bf16[16,4096]{1,0:T(8,128)(2,1)} %query_in.1, bf16[16,512]{1,0:T(8,128)(2,1)} %bitcast.8, bf16[16,256,256]{2,1,0:T(8,128)(2,1)} %keys_in.1, bf16[16,256,256]{2,1,0:T(8,128)(2,1)} %values_in.1, s32[1,16]{1,0:T(1,128)} %bitcast.13, ...), custom_call_target="tpu_custom_call" | custom-call | tf_op jit(solution)/shard_map/layer/pallas_call | solution.py:543
  94.9 1.6 %copy.19 = bf16[16,4096]{1,0:T(8,128)(2,1)} copy(bf16[16,4096]{1,0:T(8,128)(2,1)} %get-tuple-element.4) | data formatting | bytes 262144
  96.5 1.6 %copy.20 = bf16[16,4096]{1,0:T(8,128)(2,1)} copy(bf16[16,4096]{1,0:T(8,128)(2,1)} %get-tuple-element.5) | data formatting | bytes 262144

commit v3 on v2

--- a/solution.py
+++ b/solution.py
@@ -15,7 +15,11 @@
 SIDE = 4
 PLANE = 2 * SIDE * SIDE
 GROUPS = ((0, 1280), (1280, 1536), (2816, 1280))
-PARTS = (((0, 384), (0, 384), (0, 384)), ((384, 256), (384, 384), (384, 256)))
+PARTS = (
+    ((0, 256), (0, 256), (0, 256)),
+    ((256, 256), (256, 256), (256, 256)),
+    ((512, 128), (512, 256), (512, 128)),
+)
 
 
 def place():
@@ -115,15 +119,16 @@
 
 
 def kernel(
-    residual_in, query_in, new_in, keys_in, values_in, lengths, q_gain, k_gain, weight, moe_gain, ids, probs,
-    gate_up, down, attended, mixed,
-    query, keys, values, residual, scores, products_pv, heads, columns_held, blocks, products, projected,
+    residual_in, query_in, new_in, keys_in, values_in, lengths_in, q_gain_in, k_gain_in, weight, moe_gain_in,
+    ids_in, probs_in, gate_up, down, out,
+    query, keys, values, residual, new, lengths, q_gain, k_gain, moe_gain, ids, probs, scores, products_pv, heads, columns_held, blocks, products, projected,
     normed, gate_up_held, down_held, meta, shared, picked, received, total, answers, returned,
     partial, landed, choose, weigh, gather, spread,
     cache_sems, head_weight_sems, first_send, first_recv, second_send, second_recv, back_send, back_recv,
     weight_sems, meta_send, meta_recv, share_send, share_recv, out_send, out_recv,
     ret_send, ret_recv, sum_send, sum_recv,
 ):
+    attended, mixed = out.at[0], out.at[1]
     x, y, z, core = place()
     along = (x, y, z)
     across = ((y, z), (z, x), (y, x))
@@ -163,7 +168,11 @@
     loads = [
         pltpu.make_async_copy(source, target, cache_sems.at[i])
         for i, (source, target) in enumerate(
-            ((query_in, query), (keys_in, keys), (values_in, values), (residual_in, residual))
+            (
+                (query_in, query), (keys_in, keys), (values_in, values), (residual_in, residual),
+                (new_in, new), (lengths_in, lengths), (q_gain_in, q_gain), (k_gain_in, k_gain),
+                (moe_gain_in, moe_gain), (ids_in, ids), (probs_in, probs),
+            )
         )
     ]
     for load in loads:
@@ -171,7 +180,18 @@
     half = pl.ds(pl.multiple_of(core * 128, 128), 128)
     own_weight = pltpu.make_async_copy(weight, columns_held.at[:, half], head_weight_sems.at[0])
     own_weight.start()
-    each_partner(lambda axis, p: signal(in_plane(axis, p)))
+    def greet(i):
+        other = (z * SIDE + x + i) % (SIDE * SIDE)
+        signal(device(other % SIDE, y, other // SIDE, core))
+
+    def greet_row(i):
+        row = (y + i) % SIDE
+        signal(device(x, row, z, core))
+        signal(device(x, row, z, 1 - core))
+
+    signal(device(x, y, z, 1 - core))
+    loop(1, SIDE * SIDE, greet)
+    loop(1, SIDE, greet_row)
     rows_of = [pl.ds(*group) for group in GROUPS]
     fetches = [
         pltpu.make_async_copy(gate_up.at[0, rows], gate_up_held.at[rows], weight_sems.at[i])
@@ -182,6 +202,8 @@
     ]
     for fetch in fetches:
         fetch.start()
+    for load in loads[4:]:
+        load.wait()
     own_meta = route(ids[...], probs[...])
     for axis in axes:
         meta[axis, along[axis]] = own_meta
@@ -218,7 +240,7 @@
         ).astype(jnp.float32)
         rotated = exact(swap, turned(stack, many_cosines, many_sines, q_gain[...]))
         new_key = turned(
-            new_in[:, kv * 128 : kv * 128 + 128].astype(jnp.float32), cosines, sines, k_gain[...]
+            new[:, 0, kv * 128 : kv * 128 + 128].astype(jnp.float32), cosines, sines, k_gain[...]
         )
         own = jnp.sum(rotated * exact(same_token, new_key), axis=-1, keepdims=True) * scale
         queries.append(rotated.astype(jnp.bfloat16))
@@ -246,7 +268,7 @@
             products_pv[t * group : (t + 1) * group] = exact(
                 probs_of[t * group : (t + 1) * group], values[t, :, lanes_of]
             )
-        new_value = exact(same_token, new_in[:, 256 + kv * 128 : 384 + kv * 128])
+        new_value = exact(same_token, new[:, 1, kv * 128 : kv * 128 + 128])
         result = (products_pv[...] + own_prob * new_value).astype(jnp.bfloat16)
         result = exact(swap, result).astype(jnp.bfloat16)
         for h in range(group):
@@ -288,7 +310,7 @@
 
     sibling = device(x, y, z, 1 - core)
     attend(0)
-    pl.semaphore_wait(pltpu.get_barrier_semaphore(), 3 * (PLANE - 1))
+    pl.semaphore_wait(pltpu.get_barrier_semaphore(), SIDE * SIDE + 2 * (SIDE - 1))
     start_first(0)
     start_second(0, first, heads.at[:, side(0)])
     attend(1)
@@ -402,13 +424,20 @@
         ))
         shared[along[axis], :, columns(axis)] = normed[:, columns(axis)]
 
+    def dispatch(part, axis):
+        loop(1, PLANE, lambda i: send(
+            picked.at[partner(axis, i), :, lanes(part, axis)], received.at[index[axis], :, lanes(part, axis)],
+            out_send.at[part, axis], out_recv.at[part, axis], in_plane(axis, partner(axis, i)),
+        ))
+
     for axis in axes:
         to_line(axis, lambda f: wait(shared.at[0, :, columns(axis)], share_recv.at[axis, f]))
         rows = shared[:, :, columns(axis)].reshape(SIDE * 16, GROUPS[axis][1])
         result = jnp.dot(choose[axis], rows, preferred_element_type=jnp.float32)
         base, width = GROUPS[axis]
         picked[:, :, pl.ds(base // 2, width // 2)] = halves(result)
-    for part in range(len(PARTS)):
+        dispatch(0, axis)
+    for part in range(1, len(PARTS)):
         each_partner(lambda axis, p: send(
             picked.at[p, :, lanes(part, axis)], received.at[index[axis], :, lanes(part, axis)],
             out_send.at[part, axis], out_recv.at[part, axis], in_plane(axis, p),
@@ -532,7 +561,7 @@
     hidden = expert_down.shape[1]
     slots = cached_key_rows.shape[1]
     vmem = pl.BlockSpec(memory_space=pltpu.VMEM)
-    hbm = pl.BlockSpec(memory_space=pl.ANY)
+    hbm = pl.BlockSpec(memory_space=pltpu.HBM)
     sems = pltpu.SemaphoreType.DMA
     bf16 = jnp.bfloat16
     own = pltpu.VMEM((rows, width), bf16)
@@ -540,16 +569,23 @@
     messages = pltpu.VMEM((PLANE, 16, width // 2), bf16)
     lines = pltpu.VMEM((SIDE, rows, width), bf16)
     parts = len(PARTS)
-    attended, mixed = pl.pallas_call(
+    both = pl.pallas_call(
         kernel,
-        out_shape=[jax.ShapeDtypeStruct((rows, width), bf16)] * 2,
-        in_specs=[hbm, hbm, vmem, hbm, hbm, vmem, vmem, vmem, hbm, vmem, vmem, vmem, hbm, hbm],
-        out_specs=[vmem, vmem],
+        out_shape=jax.ShapeDtypeStruct((2, rows, width), bf16),
+        in_specs=[hbm] * 14,
+        out_specs=vmem,
         scratch_shapes=[
             own,
             caches,
             caches,
             own,
+            pltpu.VMEM(new_key_value.shape, bf16),
+            pltpu.VMEM((1, rows), jnp.int32),
+            pltpu.VMEM((1, 128), jnp.float32),
+            pltpu.VMEM((1, 128), jnp.float32),
+            pltpu.VMEM((1, width), jnp.float32),
+            pltpu.VMEM((expert_ids.shape[1], rows), jnp.int32),
+            pltpu.VMEM((expert_ids.shape[1], rows), jnp.float32),
             pltpu.VMEM((2, 256, slots), jnp.float32),
             pltpu.VMEM((256, 128), jnp.float32),
             own,
@@ -573,7 +609,7 @@
             pltpu.VMEM((3, 2 * SIDE * rows, 512), bf16),
             pltpu.VMEM((3, 512, 512), bf16),
             pltpu.VMEM((3, 256, 256), bf16),
-            sems((4,)),
+            sems((11,)),
             sems((3,)),
             sems((2, SIDE)),
             sems((2, SIDE)),
@@ -598,11 +634,11 @@
         ),
         name="layer",
     )(
-        residual, query, new_key_value.reshape(rows, 512), cached_key_rows, cached_value_rows,
+        residual, query, new_key_value, cached_key_rows, cached_value_rows,
         lengths.reshape(1, rows), q_gain.reshape(1, 128), k_gain.reshape(1, 128), out_weight,
         moe_gain.reshape(1, width), expert_ids.T, gate_probs.T, expert_gate_up, expert_down,
     )
-    return (attended, mixed)
+    return (both[0], both[1])
 
 
 def solution(mesh):

time: 98.3 us -> 91.7 us (0.933)
  Pallas kernels: 92.9 us -> 89.2 us
  local copies, waits for them, and re-layouts: 4.46 us -> 1.68 us
    unnamed x3 -> x0, local copies, waits for them, and re-layouts: 4.46 us -> none
    pallas_call x1, Pallas kernels: 92.9 us -> 89.2 us  [local(): pl.pallas_call(kernel, out_shape=jax.ShapeDtypeStruct((2, rows, width), b...]
    squeeze x0 -> x1, local copies, waits for them, and re-layouts: none -> 1.68 us  [local(): return (both[0], both[1])]
where the time goes in v3:
time: 91.7 us; the launch traced here: 91.6 us
  Pallas kernels  89.2 us (97%)
  local copies, waits for them, and re-layouts  1.68 us (2%)
    pallas_call x1, Pallas kernels, local(): pl.pallas_call(kernel, out_shape=jax.ShapeDtypeStruct((2, rows, width), b...  89.2 us

profile of v3, /device:TPU:1, one launch (start us, length us, event | category | flops | bytes accessed | tf_op | source)
XLA Modules:
  0.0 91.6 jit_solution(1429392506893426849)
XLA Ops:
  0.6 89.2 %layer.1 = bf16[2,16,4096]{2,1,0:T(8,128)(2,1)} custom-call(bf16[16,4096]{1,0:T(8,128)(2,1)} %residual_in.1, bf16[16,4096]{1,0:T(8,128)(2,1)} %query_in.1, bf16[16,2,256]{2,1,0:T(2,128)(2,1)} %new_in.1, bf16[16,256,256]{2,1,0:T(8,128)(2,1)} %keys_in.1, bf16[16,256,256]{2,1,0:T(8,128)(2,1)} %values_in.1, s32[1,16]{1,0:T(1,128)} %bitcast.13, ...), custom_call_target="tpu_custom_call" | custom-call | tf_op jit(solution)/shard_map/layer/pallas_call | solution.py:572
  89.9 1.7 %slice_bitcast_fusion = (bf16[16,4096]{1,0:T(8,128)(2,1)}, bf16[16,4096]{1,0:T(8,128)(2,1)}) fusion(bf16[2,16,4096]{2,1,0:T(8,128)(2,1)} %layer.1), kind=kLoop, calls=%fused_computation | loop fusion | bytes 524288 | tf_op jit(solution)/shard_map/squeeze | solution.py:641

commit v4 on v3

--- a/solution.py
+++ b/solution.py
@@ -122,9 +122,9 @@
     residual_in, query_in, new_in, keys_in, values_in, lengths_in, q_gain_in, k_gain_in, weight, moe_gain_in,
     ids_in, probs_in, gate_up, down, out,
     query, keys, values, residual, new, lengths, q_gain, k_gain, moe_gain, ids, probs, scores, products_pv, heads, columns_held, blocks, products, projected,
-    normed, gate_up_held, down_held, meta, shared, picked, received, total, answers, returned,
+    normed, gate_up_held, down_held, meta, shared, picked, received, ordered_rows, total, answers, returned,
     partial, landed, choose, weigh, gather, spread,
-    cache_sems, head_weight_sems, first_send, first_recv, second_send, second_recv, back_send, back_recv,
+    cache_sems, head_weight_sems, first_send, first_recv, second_send, second_recv, relay_send, back_send, back_recv,
     weight_sems, meta_send, meta_recv, share_send, share_recv, out_send, out_recv,
     ret_send, ret_recv, sum_send, sum_recv,
 ):
@@ -175,8 +175,8 @@
             )
         )
     ]
-    for load in loads:
-        load.start()
+    for i in (0, 4, 5, 6, 7, 1, 2, 9, 10, 8, 3):
+        loads[i].start()
     half = pl.ds(pl.multiple_of(core * 128, 128), 128)
     own_weight = pltpu.make_async_copy(weight, columns_held.at[:, half], head_weight_sems.at[0])
     own_weight.start()
@@ -192,22 +192,24 @@
     signal(device(x, y, z, 1 - core))
     loop(1, SIDE * SIDE, greet)
     loop(1, SIDE, greet_row)
-    rows_of = [pl.ds(*group) for group in GROUPS]
-    fetches = [
-        pltpu.make_async_copy(gate_up.at[0, rows], gate_up_held.at[rows], weight_sems.at[i])
-        for i, rows in enumerate(rows_of)
-    ] + [
-        pltpu.make_async_copy(down.at[0, :, rows], down_held.at[:, rows], weight_sems.at[3 + i])
-        for i, rows in enumerate(rows_of)
+    order, place_of = [], {}
+    for part in range(len(PARTS)):
+        for axis in axes:
+            for h, cols in enumerate(both_columns(part, axis)):
+                place_of[part, axis, h] = pl.ds(sum(c.size for c in order), cols.size)
+                order.append(cols)
+    gate_up_fetches = [
+        pltpu.make_async_copy(gate_up.at[0, cols], gate_up_held.at[to], weight_sems.at[3 + i])
+        for i, (cols, to) in enumerate(zip(order, place_of.values()))
+    ]
+    fetches = gate_up_fetches + [
+        pltpu.make_async_copy(down.at[0, :, cols], down_held.at[:, cols], weight_sems.at[i])
+        for i, cols in enumerate([pl.ds(*group) for group in GROUPS])
     ]
     for fetch in fetches:
         fetch.start()
-    for load in loads[4:]:
+    for load in loads[4:8]:
         load.wait()
-    own_meta = route(ids[...], probs[...])
-    for axis in axes:
-        meta[axis, along[axis]] = own_meta
-
     tokens, slots, group = 16, keys.shape[1], 16
     pairs = tokens * group
     nt = (((1,), (1,)), ((), ()))
@@ -233,8 +235,8 @@
     many_cosines = jnp.concatenate([cosines] * group, axis=0)
     many_sines = jnp.concatenate([sines] * group, axis=0)
     loads[0].wait()
-    queries, own_scores = [], []
-    for kv in range(2):
+
+    def score(kv):
         stack = jnp.concatenate(
             [query[:, (kv * group + h) * 128 : (kv * group + h + 1) * 128] for h in range(group)], axis=0
         ).astype(jnp.float32)
@@ -243,20 +245,18 @@
             new[:, 0, kv * 128 : kv * 128 + 128].astype(jnp.float32), cosines, sines, k_gain[...]
         )
         own = jnp.sum(rotated * exact(same_token, new_key), axis=-1, keepdims=True) * scale
-        queries.append(rotated.astype(jnp.bfloat16))
-        own_scores.append(own)
-    loads[1].wait()
-    for kv in range(2):
-        lanes_of = slice(kv * 128, kv * 128 + 128)
+        queries = rotated.astype(jnp.bfloat16)
+        if kv == 0:
+            loads[1].wait()
         for t in range(tokens):
             scores[kv, t * group : (t + 1) * group] = exact(
-                queries[kv][t * group : (t + 1) * group], keys[t, :, lanes_of], nt
+                queries[t * group : (t + 1) * group], keys[t, :, kv * 128 : kv * 128 + 128], nt
             )
-    loads[2].wait()
+        return own
 
     def attend(kv):
         lanes_of = slice(kv * 128, kv * 128 + 128)
-        own = own_scores[kv]
+        own = score(kv)
         masked = jnp.where(live, scores[kv] * scale, -jnp.inf)
         highest = jnp.maximum(jnp.max(masked, axis=-1, keepdims=True), own)
         expos = jnp.exp(masked - highest)
@@ -264,6 +264,8 @@
         sums = jnp.sum(expos, axis=-1, keepdims=True) + own_expo
         probs_of = (expos / sums).astype(jnp.bfloat16)
         own_prob = (own_expo / sums).astype(jnp.bfloat16).astype(jnp.float32)
+        if kv == 0:
+            loads[2].wait()
         for t in range(tokens):
             products_pv[t * group : (t + 1) * group] = exact(
                 probs_of[t * group : (t + 1) * group], values[t, :, lanes_of]
@@ -306,7 +308,7 @@
                 second_recv.at[kv, second, f], at(first, s),
             )
 
-        loop(0, SIDE - 1, one)
+        loop(0, 2, one)
 
     sibling = device(x, y, z, 1 - core)
     attend(0)
@@ -317,6 +319,12 @@
     start_first(1)
     start_second(1, first, heads.at[:, side(1)])
     send(weight, columns_held.at[:, half], head_weight_sems.at[1], head_weight_sems.at[2], sibling)
+
+    loads[9].wait()
+    loads[10].wait()
+    own_meta = route(ids[...], probs[...])
+    for axis in axes:
+        meta[axis, along[axis]] = own_meta
 
     def to_line(axis, body):
         def one(i):
@@ -338,6 +346,18 @@
             start_second(kv, f, blocks.at[second, f, :, side(kv)])
 
         loop(0, SIDE - 1, pass_on)
+    before, after = (second + SIDE - 1) % SIDE, (second + 1) % SIDE
+
+    def relay(kv, f):
+        origin, to = ((before, after), (after, before))[kv]
+        piece = blocks.at[origin, f, :, side(kv)]
+        wait(piece, second_recv.at[kv, origin, f])
+        send(piece, piece, relay_send.at[kv, f], second_recv.at[kv, origin, f], at(first, to))
+
+    for kv in range(2):
+        relay(kv, first)
+    for kv in range(2):
+        loop(0, SIDE - 1, lambda i: relay(kv, (first + near_first(i)) % SIDE))
     own_weight.wait()
     wait(weight, head_weight_sems.at[2])
     mine = pl.ds(pl.multiple_of((z * SIDE + x) * 256, 256), 256)
@@ -357,9 +377,9 @@
     loop(0, SIDE - 1, lambda i: back((first + near_first(i)) % SIDE, second))
 
     for axis in axes:
-        q = iota((1, 512), 1)
-        target = ordered(axis, q >> 4, shifted(q, 1, SIDE), q & 1) + shifted(q, 3, 2) * 256
-        gather[axis] = ones_where(iota((512, 512), 0) == target)
+        q = iota((1, 256), 1)
+        target = ordered(axis, q >> 3, shifted(q, 1, SIDE), q & 1)
+        gather[axis] = ones_where(iota((256, 256), 0) == target)
         q = iota((256, 1), 0)
         target = ordered(axis, q >> 3, shifted(q, 1, SIDE), q & 1)
         spread[axis] = ones_where(iota((256, 256), 1) == target)
@@ -388,18 +408,15 @@
             [jnp.where(upper, scaled, 0.0), jnp.where(upper, 0.0, scaled)], axis=0
         ).astype(jnp.bfloat16)
 
-    def other_group(i):
-        s = (second + near_first(i)) % SIDE
-
-        def arrived(f):
-            for kv in range(2):
-                wait(blocks.at[s, f, :, side(kv)], second_recv.at[kv, s, f])
-
-        loop(0, SIDE, arrived)
+    def group_of(s, halves_left):
+        for kv in halves_left:
+            loop(0, SIDE, lambda f: wait(blocks.at[s, f, :, side(kv)], second_recv.at[kv, s, f]))
         project(s)
         loop(0, SIDE, lambda f: back(f, s))
 
-    loop(0, SIDE - 1, other_group)
+    group_of(before, (1,))
+    group_of(after, (0,))
+    group_of((second + 2) % SIDE, (0, 1))
 
     def others_in_plane(body):
         def one(i):
@@ -410,6 +427,7 @@
 
     others_in_plane(lambda f, s: wait(products.at[s, f], back_recv.at[s, f]))
     loads[3].wait()
+    loads[8].wait()
     added = residual[...].astype(jnp.float32) + projected[...].astype(jnp.float32)
     rounded = added.astype(jnp.bfloat16)
     attended[...] = rounded
@@ -452,32 +470,33 @@
     for part in range(len(PARTS)):
         for axis in axes:
             wait(received.at[many, :, lanes(part, axis)], out_recv.at[part, axis])
+            size = PARTS[part][axis][1]
+            messages = received[:, :, lanes(part, axis)].astype(jnp.float32)
+            for h in range(2):
+                rows = messages[:, h * 8 : h * 8 + 8].reshape(PLANE * 8, size).astype(jnp.bfloat16)
+                rows = jnp.dot(gather[axis], rows, preferred_element_type=jnp.float32)
+                ordered_rows[:, place_of[part, axis, h]] = rows.astype(jnp.bfloat16)
+        for fetch in gate_up_fetches[6 * part : 6 * part + 6]:
+            fetch.wait()
+        start = place_of[part, 0, 0].start
+        depth = pl.ds(start, 2 * sum(p[1] for p in PARTS[part]))
+
+        def step(n):
+            piece = pl.ds(pl.multiple_of(n * 768, 768), 768)
+            product = jnp.dot(
+                ordered_rows[:, depth], gate_up_held[depth, piece], preferred_element_type=jnp.float32
+            )
             if part == 0:
-                fetches[axis].wait()
-            size = PARTS[part][axis][1]
-            messages = received[:, :, lanes(part, axis)].reshape(PLANE * 16, size)
-            rows = jnp.dot(gather[axis], messages, preferred_element_type=jnp.float32)
-            rows = rows.astype(jnp.bfloat16)
-            upper, lower = both_columns(part, axis)
-
-            def step(n):
-                piece = pl.ds(pl.multiple_of(n * 512, 512), 512)
-                product = jnp.dot(
-                    rows[:256], gate_up_held[upper, piece], preferred_element_type=jnp.float32
-                ) + jnp.dot(
-                    rows[256:], gate_up_held[lower, piece], preferred_element_type=jnp.float32
-                )
-                if part == 0 and axis == 0:
-                    total[:, piece] = product
-                else:
-                    total[:, piece] += product
-
-            loop(0, 2 * hidden_size // 512, step)
+                total[:, piece] = product
+            else:
+                total[:, piece] += product
+
+        loop(0, 2 * hidden_size // 768, step)
 
     gate = total[:, :hidden_size]
     hidden = (gate / (1.0 + jnp.exp(-gate)) * total[:, hidden_size:]).astype(jnp.bfloat16)
     for axis in axes:
-        fetches[3 + axis].wait()
+        fetches[len(order) + axis].wait()
     hiddens = [
         jnp.dot(spread[axis], hidden, preferred_element_type=jnp.float32).astype(jnp.bfloat16)
         for axis in axes
@@ -524,13 +543,10 @@
 
     wait(weight, head_weight_sems.at[1])
     for kv in range(2):
-        def finish_first(i):
-            f = (first + 1 + i) % SIDE
-            s = (second + 1 + i) % SIDE
-            wait(heads.at[:, side(kv)], first_send.at[kv, f])
+        loop(1, SIDE, lambda i: wait(heads.at[:, side(kv)], first_send.at[kv, (first + i) % SIDE]))
+        for s in (before, after):
             loop(0, SIDE, lambda g: wait(heads.at[:, side(kv)], second_send.at[kv, s, g]))
-
-        loop(0, SIDE - 1, finish_first)
+        loop(0, SIDE, lambda g: wait(heads.at[:, side(kv)], relay_send.at[kv, g]))
     others_in_plane(lambda f, s: wait(products.at[s, f], back_send.at[s, f]))
     for axis in axes:
         to_line(axis, lambda f: wait(meta.at[axis, 0], meta_send.at[axis, f]))
@@ -600,6 +616,7 @@
             lines,
             messages,
             messages,
+            pltpu.VMEM((256, width), bf16),
             pltpu.VMEM((256, 2 * hidden), jnp.float32),
             messages,
             messages,
@@ -607,7 +624,7 @@
             lines,
             pltpu.VMEM((3, 256, SIDE * rows), bf16),
             pltpu.VMEM((3, 2 * SIDE * rows, 512), bf16),
-            pltpu.VMEM((3, 512, 512), bf16),
+            pltpu.VMEM((3, 256, 256), bf16),
             pltpu.VMEM((3, 256, 256), bf16),
             sems((11,)),
             sems((3,)),
@@ -615,9 +632,10 @@
             sems((2, SIDE)),
             sems((2, SIDE, SIDE)),
             sems((2, SIDE, SIDE)),
+            sems((2, SIDE)),
             sems((SIDE, SIDE)),
             sems((SIDE, SIDE)),
-            sems((6,)),
+            sems((3 + 6 * parts,)),
             sems((3, SIDE)),
             sems((3, SIDE)),
             sems((3, SIDE)),

time: 91.7 us -> 86.9 us (0.948)
  Pallas kernels: 89.2 us -> 84.5 us
    pallas_call x1, Pallas kernels: 89.2 us -> 84.5 us  [local(): pl.pallas_call(kernel, out_shape=jax.ShapeDtypeStruct((2, rows, width), b...]
where the time goes in v4:
time: 86.9 us; the launch traced here: 86.8 us
  Pallas kernels  84.5 us (97%)
  local copies, waits for them, and re-layouts  1.68 us (2%)
    pallas_call x1, Pallas kernels, local(): pl.pallas_call(kernel, out_shape=jax.ShapeDtypeStruct((2, rows, width), b...  84.5 us

profile of v4, /device:TPU:1, one launch (start us, length us, event | category | flops | bytes accessed | tf_op | source)
XLA Modules:
  0.0 86.8 jit_solution(12565533245981559688)
XLA Ops:
  0.6 84.5 %layer.1 = bf16[2,16,4096]{2,1,0:T(8,128)(2,1)} custom-call(bf16[16,4096]{1,0:T(8,128)(2,1)} %residual_in.1, bf16[16,4096]{1,0:T(8,128)(2,1)} %query_in.1, bf16[16,2,256]{2,1,0:T(2,128)(2,1)} %new_in.1, bf16[16,256,256]{2,1,0:T(8,128)(2,1)} %keys_in.1, bf16[16,256,256]{2,1,0:T(8,128)(2,1)} %values_in.1, s32[1,16]{1,0:T(1,128)} %bitcast.13, ...), custom_call_target="tpu_custom_call" | custom-call | tf_op jit(solution)/shard_map/layer/pallas_call | solution.py:588
  85.1 1.7 %slice_bitcast_fusion = (bf16[16,4096]{1,0:T(8,128)(2,1)}, bf16[16,4096]{1,0:T(8,128)(2,1)}) fusion(bf16[2,16,4096]{2,1,0:T(8,128)(2,1)} %layer.1), kind=kLoop, calls=%fused_computation | loop fusion | bytes 524288 | tf_op jit(solution)/shard_map/squeeze | solution.py:659

commit v5 on v4

--- a/solution.py
+++ b/solution.py
@@ -142,7 +142,7 @@
         return device(*spot(axis, p // (2 * SIDE), (p // 2) % SIDE, along[axis]), p % 2)
 
     def partner(axis, i):
-        step = (13 * i) % PLANE
+        step = (27 * i) % PLANE
         a, b = across[axis]
         return (((a + step // (2 * SIDE)) % SIDE) * SIDE + (b + step // 2) % SIDE) * 2 + (core + step) % 2
 
@@ -181,17 +181,13 @@
     own_weight = pltpu.make_async_copy(weight, columns_held.at[:, half], head_weight_sems.at[0])
     own_weight.start()
     def greet(i):
-        other = (z * SIDE + x + i) % (SIDE * SIDE)
-        signal(device(other % SIDE, y, other // SIDE, core))
-
-    def greet_row(i):
-        row = (y + i) % SIDE
-        signal(device(x, row, z, core))
-        signal(device(x, row, z, 1 - core))
+        signal(device((x + i) % SIDE, y, z, core))
+        signal(device(x, y, (z + i) % SIDE, core))
+        signal(device(x, (y + i) % SIDE, z, core))
+        signal(device(x, (y + i) % SIDE, z, 1 - core))
 
     signal(device(x, y, z, 1 - core))
-    loop(1, SIDE * SIDE, greet)
-    loop(1, SIDE, greet_row)
+    loop(1, SIDE, greet)
     order, place_of = [], {}
     for part in range(len(PARTS)):
         for axis in axes:
@@ -312,7 +308,7 @@
 
     sibling = device(x, y, z, 1 - core)
     attend(0)
-    pl.semaphore_wait(pltpu.get_barrier_semaphore(), SIDE * SIDE + 2 * (SIDE - 1))
+    pl.semaphore_wait(pltpu.get_barrier_semaphore(), 1 + 4 * (SIDE - 1))
     start_first(0)
     start_second(0, first, heads.at[:, side(0)])
     attend(1)

time: 86.9 us -> 85.7 us (0.986)
  Pallas kernels: 84.5 us -> 83.2 us
    pallas_call x1, Pallas kernels: 84.5 us -> 83.2 us  [local(): pl.pallas_call(kernel, out_shape=jax.ShapeDtypeStruct((2, rows, width), b...]
where the time goes in v5:
time: 85.7 us; the launch traced here: 85.6 us
  Pallas kernels  83.2 us (97%)
  local copies, waits for them, and re-layouts  1.68 us (2%)
    pallas_call x1, Pallas kernels, local(): pl.pallas_call(kernel, out_shape=jax.ShapeDtypeStruct((2, rows, width), b...  83.2 us

profile of v5, /device:TPU:1, one launch (start us, length us, event | category | flops | bytes accessed | tf_op | source)
XLA Modules:
  0.0 85.6 jit_solution(11359181699948343135)
XLA Ops:
  0.6 83.2 %layer.1 = bf16[2,16,4096]{2,1,0:T(8,128)(2,1)} custom-call(bf16[16,4096]{1,0:T(8,128)(2,1)} %residual_in.1, bf16[16,4096]{1,0:T(8,128)(2,1)} %query_in.1, bf16[16,2,256]{2,1,0:T(2,128)(2,1)} %new_in.1, bf16[16,256,256]{2,1,0:T(8,128)(2,1)} %keys_in.1, bf16[16,256,256]{2,1,0:T(8,128)(2,1)} %values_in.1, s32[1,16]{1,0:T(1,128)} %bitcast.13, ...), custom_call_target="tpu_custom_call" | custom-call | tf_op jit(solution)/shard_map/layer/pallas_call | solution.py:584
  83.9 1.7 %slice_bitcast_fusion = (bf16[16,4096]{1,0:T(8,128)(2,1)}, bf16[16,4096]{1,0:T(8,128)(2,1)}) fusion(bf16[2,16,4096]{2,1,0:T(8,128)(2,1)} %layer.1), kind=kLoop, calls=%fused_computation | loop fusion | bytes 524288 | tf_op jit(solution)/shard_map/squeeze | solution.py:655

commit v6 on v5

--- a/solution.py
+++ b/solution.py
@@ -487,10 +487,15 @@
             else:
                 total[:, piece] += product
 
-        loop(0, 2 * hidden_size // 768, step)
-
-    gate = total[:, :hidden_size]
-    hidden = (gate / (1.0 + jnp.exp(-gate)) * total[:, hidden_size:]).astype(jnp.bfloat16)
+        if part < len(PARTS) - 1:
+            loop(0, 2 * hidden_size // 768, step)
+
+    gate, up = [
+        total[:, piece]
+        + jnp.dot(ordered_rows[:, depth], gate_up_held[depth, piece], preferred_element_type=jnp.float32)
+        for piece in (pl.ds(0, hidden_size), pl.ds(hidden_size, hidden_size))
+    ]
+    hidden = (gate / (1.0 + jnp.exp(-gate)) * up).astype(jnp.bfloat16)
     for axis in axes:
         fetches[len(order) + axis].wait()
     hiddens = [

time: 85.7 us -> 85.2 us (level)
  no operation moved by 1% of the time
where the time goes in v6:
time: 85.2 us; the launch traced here: 85.1 us
  Pallas kernels  82.8 us (97%)
  local copies, waits for them, and re-layouts  1.68 us (2%)
    pallas_call x1, Pallas kernels, local(): pl.pallas_call(kernel, out_shape=jax.ShapeDtypeStruct((2, rows, width), b...  82.8 us

profile of v6, /device:TPU:1, one launch (start us, length us, event | category | flops | bytes accessed | tf_op | source)
XLA Modules:
  0.0 85.1 jit_solution(17360577818978205396)
XLA Ops:
  0.6 82.8 %layer.1 = bf16[2,16,4096]{2,1,0:T(8,128)(2,1)} custom-call(bf16[16,4096]{1,0:T(8,128)(2,1)} %residual_in.1, bf16[16,4096]{1,0:T(8,128)(2,1)} %query_in.1, bf16[16,2,256]{2,1,0:T(2,128)(2,1)} %new_in.1, bf16[16,256,256]{2,1,0:T(8,128)(2,1)} %keys_in.1, bf16[16,256,256]{2,1,0:T(8,128)(2,1)} %values_in.1, s32[1,16]{1,0:T(1,128)} %bitcast.13, ...), custom_call_target="tpu_custom_call" | custom-call | tf_op jit(solution)/shard_map/layer/pallas_call | solution.py:589
  83.4 1.7 %slice_bitcast_fusion = (bf16[16,4096]{1,0:T(8,128)(2,1)}, bf16[16,4096]{1,0:T(8,128)(2,1)}) fusion(bf16[2,16,4096]{2,1,0:T(8,128)(2,1)} %layer.1), kind=kLoop, calls=%fused_computation | loop fusion | bytes 524288 | tf_op jit(solution)/shard_map/squeeze | solution.py:660
